TPU v7x, 512 devices: a whole 4x8x8 slice. The times are simulated.
512 devices in a mesh: dp: 32 (over x, z), etp: 16 (over y, core).
Axes of the slice: x: 4, y: 8, z: 8, core: 2. Of those that a mesh axis runs over, the one named last changes fastest.
Arguments:
- momentum: float32 [32, 3584, 1536], P('dp', 'etp'), may hold values from -6 to 6
- grad: bfloat16 [32, 3584, 1536], P('dp', 'etp'), may hold values from -3100 to 3100
- q_in: float32 [32, 1536, 64], P('dp'), may hold values from -0.15625 to 0.15625
Outputs:
- momentum_out: float32 [32, 3584, 1536], P('dp', 'etp')
- q_out: float32 [32, 1536, 64], P('dp')
- update: bfloat16 [32, 3584, 1536], P('dp', 'etp')
All inputs are finite; a program needn't handle non-finite values.
Results may differ from a plain program's by a relative error of at most 0.0045.
Values sent between devices are 32-bit elements; how exact they have to be, the bound alone decides.
A program may use at most 64 MiB of HBM per device.

v0:
```python
import math

import jax
import jax.numpy as jnp
from jax import lax
from jax.sharding import PartitionSpec as P

ROWS = 3584
COLS = 1536
RANK = 64
ITERS = 8


keep_rate = 0.9
epsilon = 1e-06


def product(pattern, former, latter):
    return jnp.einsum(
        pattern, former, latter, precision=lax.Precision.HIGHEST, preferred_element_type=jnp.float32
    )


def solve_right(lower_factor, matrix):
    return lax.linalg.triangular_solve(
        lower_factor, matrix, left_side=False, lower=True, transpose_a=True
    )


def body(momentum, grad, q_in):
    etp_size = lax.axis_size("etp")
    column_count = grad.shape[2]
    element_count = float(
        grad.shape[0] * lax.axis_size("dp") * grad.shape[1] * etp_size * column_count
    )
    grad_wide = grad.astype(jnp.float32)
    total_sq = lax.psum(jnp.sum(grad_wide * grad_wide), ("dp", "etp"))
    clip_factor = jnp.minimum(1.0, lax.rsqrt(total_sq / element_count + epsilon))
    blended = momentum + clip_factor * grad_wide
    right_basis = q_in
    raw_left = product("erc,eck->erk", blended, q_in)
    left_basis = raw_left
    column_sq = jnp.zeros((q_in.shape[0], q_in.shape[2]), jnp.float32)
    for turn_index in range(ITERS):
        final_turn = turn_index + 1 == ITERS
        gram_matrix = lax.psum(product("erk,erl->ekl", raw_left, raw_left), "etp")
        lower_factor = jnp.linalg.cholesky(gram_matrix)
        left_basis = solve_right(lower_factor, raw_left)
        across = lax.psum(product("erc,erk->eck", blended, left_basis), "etp")
        column_sq = jnp.sum(across * across, axis=1)
        right_piece = across * lax.rsqrt(column_sq + epsilon)[:, None, :]
        right_basis = right_piece
        if not final_turn:
            raw_left = product("erc,eck->erk", blended, right_basis)
    norms = jnp.sqrt(column_sq + epsilon)
    momentum_new = blended - (1.0 - keep_rate) * product(
        "erk,eck->erc", left_basis * norms[:, None, :], right_basis
    )
    update_scale = math.sqrt(ROWS * COLS / RANK)
    update_new = (update_scale * product("erk,eck->erc", left_basis, right_basis)).astype(
        jnp.bfloat16
    )
    return (momentum_new, right_basis, update_new)


def solution(mesh):
    return jax.shard_map(
        body,
        mesh=mesh,
        in_specs=(P("dp", "etp", None), P("dp", "etp", None), P("dp", None, None)),
        out_specs=(P("dp", "etp", None), P("dp", None, None), P("dp", "etp", None)),
        check_vma=False,
    )
```

profile of v0, /device:TPU:1, one launch (start us, length us, event | category | flops | bytes accessed | tf_op | source)
XLA Modules:
  0.0 1564.2 jit_solution(16971271727469958371)
XLA Ops:
  7.2 2.1 fusion.4
  9.3 106.1 %psum.119 = f32[]{:T(128)} all-reduce(f32[]{:T(128)} %fusion.4), channel_id=1, replica_groups=mesh['dp'=32,'etp'=16] {'dp','etp'}, use_global_device_ids=true, to_apply=%region_1.0 | all-reduce | flops 1 | bytes 8 | tf_op jit(solution)/shard_map/psum | solution.py:37
  119.4 43.5 %psum.120 = f32[1,64,64]{1,2,0:T(8,128)S(1)} all-reduce(f32[1,64,64]{1,2,0:T(8,128)S(1)} %convolution_bitcast_fusion.22), channel_id=1, replica_groups=mesh['dp'=32,'etp'=16] {'etp'}, use_global_device_ids=true, to_apply=%region_2.0 | all-reduce | flops 4096 | bytes 32768 | tf_op jit(solution)/shard_map/psum | solution.py:46
  163.0 5.8 custom-call.20
  170.2 4.9 custom-call.21
  177.2 111.4 %all-reduce.9.cloned.1.call-done = f32[1,1536,64]{1,2,0:T(8,128)} async-done(((f32[1,1536,64]{1,2,0:T(8,128)}), f32[1,1536,64]{1,2,0:T(8,128)}) %all-reduce.9.cloned.1.call-update) | async-done | bytes 393232 | tf_op jit(solution)/shard_map/psum | solution.py:49
  289.7 2.4 fusion.25
  292.4 45.6 %psum.122 = f32[1,64,64]{1,2,0:T(8,128)S(1)} all-reduce(f32[1,64,64]{1,2,0:T(8,128)S(1)} %convolution_bitcast_fusion.21), channel_id=1, replica_groups=mesh['dp'=32,'etp'=16] {'etp'}, use_global_device_ids=true, to_apply=%region_7.10 | all-reduce | flops 4096 | bytes 32768 | tf_op jit(solution)/shard_map/psum | solution.py:46
  338.0 5.8 custom-call.22
  345.2 4.9 custom-call.23
  350.4 1.8 convolution_bitcast_fusion.6
  352.2 116.5 %all-reduce.11.cloned.1.call-done = f32[1,1536,64]{1,2,0:T(8,128)} async-done(((f32[1,1536,64]{1,2,0:T(8,128)}), f32[1,1536,64]{1,2,0:T(8,128)}) %all-reduce.11.cloned.1.call-update) | async-done | bytes 393232 | tf_op jit(solution)/shard_map/psum | solution.py:49
  469.9 2.4 fusion.22
  472.5 45.8 %psum.124 = f32[1,64,64]{1,2,0:T(8,128)S(1)} all-reduce(f32[1,64,64]{1,2,0:T(8,128)S(1)} %convolution_bitcast_fusion.20), channel_id=1, replica_groups=mesh['dp'=32,'etp'=16] {'etp'}, use_global_device_ids=true, to_apply=%region_10.13 | all-reduce | flops 4096 | bytes 32768 | tf_op jit(solution)/shard_map/psum | solution.py:46
  518.4 5.8 custom-call.24
  525.6 4.9 custom-call.25
  532.6 116.5 %all-reduce.13.cloned.1.call-done = f32[1,1536,64]{1,2,0:T(8,128)} async-done(((f32[1,1536,64]{1,2,0:T(8,128)}), f32[1,1536,64]{1,2,0:T(8,128)}) %all-reduce.13.cloned.1.call-update) | async-done | bytes 393232 | tf_op jit(solution)/shard_map/psum | solution.py:49
  650.2 2.4 fusion.19
  652.9 45.6 %psum.126 = f32[1,64,64]{1,2,0:T(8,128)S(1)} all-reduce(f32[1,64,64]{1,2,0:T(8,128)S(1)} %convolution_bitcast_fusion.19), channel_id=1, replica_groups=mesh['dp'=32,'etp'=16] {'etp'}, use_global_device_ids=true, to_apply=%region_13.16 | all-reduce | flops 4096 | bytes 32768 | tf_op jit(solution)/shard_map/psum | solution.py:46
  698.5 5.8 custom-call.26
  705.7 4.9 custom-call.27
  710.9 1.8 convolution_bitcast_fusion.4
  712.7 116.5 %all-reduce.15.cloned.1.call-done = f32[1,1536,64]{1,2,0:T(8,128)} async-done(((f32[1,1536,64]{1,2,0:T(8,128)}), f32[1,1536,64]{1,2,0:T(8,128)}) %all-reduce.15.cloned.1.call-update) | async-done | bytes 393232 | tf_op jit(solution)/shard_map/psum | solution.py:49
  830.3 2.4 fusion.16
  833.0 45.6 %psum.128 = f32[1,64,64]{1,2,0:T(8,128)S(1)} all-reduce(f32[1,64,64]{1,2,0:T(8,128)S(1)} %convolution_bitcast_fusion.18), channel_id=1, replica_groups=mesh['dp'=32,'etp'=16] {'etp'}, use_global_device_ids=true, to_apply=%region_16.19 | all-reduce | flops 4096 | bytes 32768 | tf_op jit(solution)/shard_map/psum | solution.py:46
  878.6 5.8 custom-call.28
  885.8 4.9 custom-call.29
  891.0 1.8 convolution_bitcast_fusion.3
  893.0 116.3 %all-reduce.17.cloned.1.call-done = f32[1,1536,64]{1,2,0:T(8,128)} async-done(((f32[1,1536,64]{1,2,0:T(8,128)}), f32[1,1536,64]{1,2,0:T(8,128)}) %all-reduce.17.cloned.1.call-update) | async-done | bytes 393232 | tf_op jit(solution)/shard_map/psum | solution.py:49
  1010.4 2.4 fusion.13
  1013.1 45.6 %psum.130 = f32[1,64,64]{1,2,0:T(8,128)S(1)} all-reduce(f32[1,64,64]{1,2,0:T(8,128)S(1)} %convolution_bitcast_fusion.17), channel_id=1, replica_groups=mesh['dp'=32,'etp'=16] {'etp'}, use_global_device_ids=true, to_apply=%region_19.22 | all-reduce | flops 4096 | bytes 32768 | tf_op jit(solution)/shard_map/psum | solution.py:46
  1058.7 5.8 custom-call.30
  1065.9 4.9 custom-call.31
  1071.1 1.8 convolution_bitcast_fusion.2
  1073.0 116.5 %all-reduce.19.cloned.1.call-done = f32[1,1536,64]{1,2,0:T(8,128)} async-done(((f32[1,1536,64]{1,2,0:T(8,128)}), f32[1,1536,64]{1,2,0:T(8,128)}) %all-reduce.19.cloned.1.call-update) | async-done | bytes 393232 | tf_op jit(solution)/shard_map/psum | solution.py:49
  1190.6 2.4 fusion.10
  1193.2 45.6 %psum.132 = f32[1,64,64]{1,2,0:T(8,128)S(1)} all-reduce(f32[1,64,64]{1,2,0:T(8,128)S(1)} %convolution_bitcast_fusion.16), channel_id=1, replica_groups=mesh['dp'=32,'etp'=16] {'etp'}, use_global_device_ids=true, to_apply=%region_22.25 | all-reduce | flops 4096 | bytes 32768 | tf_op jit(solution)/shard_map/psum | solution.py:46
  1238.8 5.8 custom-call.32
  1246.0 4.9 custom-call.33
  1251.2 1.8 convolution_bitcast_fusion.1
  1253.1 116.5 %all-reduce.21.cloned.1.call-done = f32[1,1536,64]{1,2,0:T(8,128)} async-done(((f32[1,1536,64]{1,2,0:T(8,128)}), f32[1,1536,64]{1,2,0:T(8,128)}) %all-reduce.21.cloned.1.call-update) | async-done | bytes 393232 | tf_op jit(solution)/shard_map/psum | solution.py:49
  1370.7 2.4 fusion.7
  1373.3 45.9 %psum.134 = f32[1,64,64]{1,2,0:T(8,128)S(1)} all-reduce(f32[1,64,64]{1,2,0:T(8,128)S(1)} %convolution_bitcast_fusion.15), channel_id=1, replica_groups=mesh['dp'=32,'etp'=16] {'etp'}, use_global_device_ids=true, to_apply=%region_25.28 | all-reduce | flops 4096 | bytes 32768 | tf_op jit(solution)/shard_map/psum | solution.py:46
  1419.3 5.8 custom-call.34
  1426.5 4.9 custom-call.35
  1433.5 116.5 %all-reduce.23.cloned.1.call-done = f32[1,1536,64]{1,2,0:T(8,128)} async-done(((f32[1,1536,64]{1,2,0:T(8,128)}), f32[1,1536,64]{1,2,0:T(8,128)}) %all-reduce.23.cloned.1.call-update) | async-done | bytes 393232 | tf_op jit(solution)/shard_map/psum | solution.py:49
  1552.2 2.1 fusion.3
  1554.4 2.5 fusion.1
  (98 shorter events, 34.3 us)
Async XLA Ops:
  7.2 110.6 %copy-start = (f32[1,1536,64]{1,2,0:T(8,128)S(1)}, f32[1,1536,64]{1,2,0:T(8,128)}, u32[]{:S(2)}) copy-start(f32[1,1536,64]{1,2,0:T(8,128)} %param.8) | copy-start | bytes 1179652
  7.2 281.4 %all-reduce.9.cloned.1.call-start = ((), (), s32[]{:S(2)}) async-start(), calls=%async_computation | async-start | bytes 786432 | tf_op jit(solution)/shard_map/psum | solution.py:49
  177.2 291.5 %all-reduce.11.cloned.1.call-start = ((), (), s32[]{:S(2)}) async-start(), calls=%async_computation.1 | async-start | bytes 786432 | tf_op jit(solution)/shard_map/psum | solution.py:49
  352.2 296.9 %all-reduce.13.cloned.1.call-start = ((), (), s32[]{:S(2)}) async-start(), calls=%async_computation.2 | async-start | bytes 786432 | tf_op jit(solution)/shard_map/psum | solution.py:49
  532.6 296.6 %all-reduce.15.cloned.1.call-start = ((), (), s32[]{:S(2)}) async-start(), calls=%async_computation.3 | async-start | bytes 786432 | tf_op jit(solution)/shard_map/psum | solution.py:49
  712.7 296.6 %all-reduce.17.cloned.1.call-start = ((), (), s32[]{:S(2)}) async-start(), calls=%async_computation.4 | async-start | bytes 786432 | tf_op jit(solution)/shard_map/psum | solution.py:49
  892.8 296.6 %all-reduce.19.cloned.1.call-start = ((), (), s32[]{:S(2)}) async-start(), calls=%async_computation.5 | async-start | bytes 786432 | tf_op jit(solution)/shard_map/psum | solution.py:49
  1072.9 296.6 %all-reduce.21.cloned.1.call-start = ((), (), s32[]{:S(2)}) async-start(), calls=%async_computation.6 | async-start | bytes 786432 | tf_op jit(solution)/shard_map/psum | solution.py:49
  1253.0 297.0 %all-reduce.23.cloned.1.call-start = ((), (), s32[]{:S(2)}) async-start(), calls=%async_computation.7 | async-start | bytes 786432 | tf_op jit(solution)/shard_map/psum | solution.py:49
  1552.2 4.7 copy-start.1
Sparse Core Ops, SparseCore 0:
  177.3 111.2 all-reduce.8
  352.3 116.3 all-reduce.10
  532.7 116.3 all-reduce.12
  712.8 116.3 all-reduce.14
  892.9 116.3 all-reduce.16
  1073.0 116.3 all-reduce.18
  1253.1 116.3 all-reduce.20
  1433.6 116.3 all-reduce.22
where the time goes:
time: 1570 us; the launch traced here: 1560 us
  waiting for transfers between devices  927 us (59%)
  blocking collectives  469 us (30%)
  other arithmetic  111 us (7%)
  matrix products  41 us (3%)
    psum x8, waiting for transfers between devices, body(): across = lax.psum(product('erc,erk->eck', blended, left_basis), 'etp')  927 us
    psum x8, blocking collectives, body(): gram_matrix = lax.psum(product('erk,erl->ekl', raw_left, raw_left), 'etp')  363 us
    psum x1, blocking collectives, body(): total_sq = lax.psum(jnp.sum(grad_wide * grad_wide), ('dp', 'etp'))  106 us
    another operation x24, other arithmetic, body(): lower_factor = jnp.linalg.cholesky(gram_matrix)  52.2 us
    another operation x16, other arithmetic, solve_right(): lax.linalg.triangular_solve(lower_factor, matrix, left_side=False, lower=...  44.4 us
    dot_general x26, matrix products, product(): jnp.einsum(pattern, former, latter, precision=lax.Precision.HIGHEST, pref...  38.9 us
  transfers between devices with their start and end apart: 8, of which 8 were waited for; matrix products, arithmetic and copies ran while one was open for 0% of the time, Pallas kernels for 0%

commit v1 on v0

v1 whole, which is shorter than its diff:
```python
import functools
import math

import jax
import jax.numpy as jnp
from jax import lax
from jax.experimental import pallas as pl
from jax.experimental.pallas import tpu as pltpu
from jax.sharding import PartitionSpec as P

ROWS = 3584
COLS = 1536
RANK = 64
ITERS = 8
DIRECT = 3

BLOCK = 128
BLOCKS = COLS // BLOCK
TILES = 5
RING = 8

keep_rate = 0.9
epsilon = 1e-06

MESH = pl.DeviceIdType.MESH
HIGHEST = lax.Precision.HIGHEST
F32 = jnp.float32
BF16 = jnp.bfloat16


def nn(former, latter, precision=None):
    return jnp.dot(former, latter, precision=precision, preferred_element_type=F32)


def nt(former, latter, precision=None):
    return lax.dot_general(
        former, latter, (((1,), (1,)), ((), ())), precision=precision, preferred_element_type=F32
    )


def split(values):
    high = values.astype(BF16)
    rest = values - high.astype(F32)
    middle = rest.astype(BF16)
    low = (rest - middle.astype(F32)).astype(BF16)
    return high, middle, low


def inverse_cholesky(gram):
    full = (8, 2 * RANK)
    ones = lax.broadcasted_iota(jnp.int32, (RANK, RANK), 0) == lax.broadcasted_iota(
        jnp.int32, (RANK, RANK), 1
    )
    joined = jnp.concatenate([gram, ones.astype(F32)], axis=1)
    panels = [joined[8 * p : 8 * p + 8] for p in range(RANK // 8)]
    sublane = lax.broadcasted_iota(jnp.int32, full, 0)
    for p in range(RANK // 8):
        panel = panels[p]
        entry = [[None] * 8 for _ in range(8)]
        for i in range(8):
            for j in range(i + 1):
                entry[i][j] = jnp.broadcast_to(panel[i : i + 1, 8 * p + j : 8 * p + j + 1], full)
        rows = [jnp.broadcast_to(panel[i : i + 1, :], full) for i in range(8)]
        scale = [None] * 8
        factor = [[None] * 8 for _ in range(8)]
        for j in range(8):
            scale[j] = lax.rsqrt(entry[j][j])
            for i in range(j + 1, 8):
                factor[i][j] = entry[i][j] * scale[j]
            for i in range(j + 1, 8):
                for m in range(j + 1, i + 1):
                    entry[i][m] = entry[i][m] - factor[i][j] * factor[m][j]
            rows[j] = rows[j] * scale[j]
            for i in range(j + 1, 8):
                rows[i] = rows[i] - factor[i][j] * rows[j]
        done = rows[0]
        for i in range(1, 8):
            done = jnp.where(sublane == i, rows[i], done)
        panels[p] = done
        for q in range(p + 1, RANK // 8):
            column = [
                jnp.broadcast_to(panels[q][:, 8 * p + j : 8 * p + j + 1], full) for j in range(8)
            ]
            for j in range(8):
                column[j] = column[j] * scale[j]
                for i in range(j + 1, 8):
                    column[i] = column[i] - factor[i][j] * column[j]
            left = panels[q]
            for j in range(8):
                left = left - column[j] * rows[j]
            panels[q] = left
    return jnp.concatenate(panels, axis=0)[:, RANK:]


def refresh_kernel(
    dp_size,
    element_count,
    m_ref,
    g_ref,
    q_ref,
    s_out,
    a_out,
    r_out,
    clip_out,
    wide,
    other_m,
    other_g,
    sums,
    totals,
    tall,
    flat,
    mine,
    ring_in,
    ring_out,
    tiles,
    sib_tiles,
    w_high,
    w_mid,
    w_low,
    r_ref,
    z_ref,
    v_ref,
    a_ref,
    small_send,
    small_recv,
    big_send,
    big_recv,
    ring_send,
    ring_recv,
    gather_send,
    gather_recv,
    sib_send,
    sib_recv,
):
    me = lax.axis_index("etp")
    dp = lax.axis_index("dp")
    etp_size = 2 * RING
    chip = me // 2
    core = lax.rem(me, 2)
    sibling = chip * 2 + (1 - core)
    way = 1 - 2 * core
    ahead = lax.rem(chip + way + RING, RING) * 2 + core
    rows = m_ref.shape[0]

    barrier = pltpu.get_barrier_semaphore()

    @pl.loop(1, etp_size)
    def _(step):
        pl.semaphore_signal(
            barrier, inc=1, device_id={"etp": lax.rem(me + step, etp_size)}, device_id_type=MESH
        )

    @pl.loop(1, dp_size)
    def _(step):
        pl.semaphore_signal(
            barrier, inc=1, device_id={"dp": lax.rem(dp + step, dp_size)}, device_id_type=MESH
        )

    wide[...] = g_ref[...].astype(F32)
    partial = jnp.zeros((8, BLOCK), F32)
    for b in range(BLOCKS):
        piece = wide[:, BLOCK * b : BLOCK * (b + 1)]
        partial = partial + jnp.sum((piece * piece).reshape(rows // 8, 8, BLOCK), axis=0)
    sums[me] = partial

    pl.semaphore_wait(barrier, etp_size + dp_size - 2)

    @pl.loop(1, etp_size)
    def _(step):
        pltpu.make_async_remote_copy(
            src_ref=sums.at[me],
            dst_ref=sums.at[me],
            send_sem=small_send.at[0],
            recv_sem=small_recv.at[0],
            device_id={"etp": lax.rem(me + step, etp_size)},
            device_id_type=MESH,
        ).start()

    copies = [
        pltpu.make_async_remote_copy(
            src_ref=source,
            dst_ref=target,
            send_sem=big_send.at[n],
            recv_sem=big_recv.at[n],
            device_id={"etp": sibling},
            device_id_type=MESH,
        )
        for n, (source, target) in enumerate(((m_ref, other_m), (wide, other_g)))
    ]
    for copy in copies:
        copy.start()

    others = sums.at[pl.ds(0, etp_size - 1)]
    pltpu.make_async_copy(others, others, small_recv.at[0]).wait()
    group = sums[0]
    for n in range(1, etp_size):
        group = group + sums[n]
    totals[dp] = group

    if dp_size > 1:

        @pl.loop(1, dp_size)
        def _(step):
            pltpu.make_async_remote_copy(
                src_ref=totals.at[dp],
                dst_ref=totals.at[dp],
                send_sem=small_send.at[1],
                recv_sem=small_recv.at[1],
                device_id={"dp": lax.rem(dp + step, dp_size)},
                device_id_type=MESH,
            ).start()

        far = totals.at[pl.ds(0, dp_size - 1)]
        pltpu.make_async_copy(far, far, small_recv.at[1]).wait()
        pltpu.make_async_copy(far, far, small_send.at[1]).wait()
    pltpu.make_async_copy(others, others, small_send.at[0]).wait()
    everything = totals[0]
    for n in range(1, dp_size):
        everything = everything + totals[n]
    total_sq = jnp.sum(jnp.sum(everything, axis=0, keepdims=True), axis=1, keepdims=True)
    clip = jnp.minimum(1.0, lax.rsqrt(total_sq / element_count + epsilon))
    clip_out[...] = jnp.broadcast_to(clip, (8, BLOCK))
    for copy in copies:
        copy.wait()

    for b in range(BLOCKS):
        columns = slice(BLOCK * b, BLOCK * (b + 1))
        own = m_ref[:, columns] + clip * wide[:, columns]
        sib = other_m[:, columns] + clip * other_g[:, columns]
        blended = jnp.concatenate([own, sib], axis=0)
        for n, part in enumerate(split(blended)):
            tall[b, :, BLOCK * n : BLOCK * (n + 1)] = part
        for n, part in enumerate(split(blended.T)):
            flat[b, BLOCK * n : BLOCK * (n + 1), :] = part

    def place(chunk, of_core, s):
        tile = TILES * (2 * chunk + of_core) + s
        row = lax.rem(tile, BLOCKS)
        return row, lax.rem(row + tile // BLOCKS, BLOCKS)

    def own_tiles(chunk):
        for s in range(TILES):
            row, column = place(chunk, core, s)
            both = nn(flat[row], tall[column])
            part = lambda i, j: both[BLOCK * i : BLOCK * (i + 1), BLOCK * j : BLOCK * (j + 1)]
            mine[s] = (
                part(0, 0) + ((part(0, 1) + part(1, 0)) + (part(1, 1) + (part(0, 2) + part(2, 0))))
            )

    def ring_copy(step, s):
        return pltpu.make_async_remote_copy(
            src_ref=ring_out.at[step, s],
            dst_ref=ring_in.at[step, s],
            send_sem=ring_send,
            recv_sem=ring_recv.at[step, s],
            device_id={"etp": ahead},
            device_id_type=MESH,
        )

    own_tiles(lax.rem(chip - way + RING, RING))
    for s in range(TILES):
        ring_out[0, s] = mine[s]
        ring_copy(0, s).start()

    @pl.loop(1, RING - 1)
    def _(step):
        own_tiles(lax.rem(chip - way * (1 + step) + 2 * RING, RING))
        for s in range(TILES):
            ring_copy(step - 1, s).wait_recv()
            ring_out[step, s] = mine[s] + ring_in[step - 1, s]
            ring_copy(step, s).start()

    def gather_copy(step, s):
        chunk = lax.rem(chip - way * step + 2 * RING, RING)
        return pltpu.make_async_remote_copy(
            src_ref=tiles.at[chunk, s],
            dst_ref=tiles.at[chunk, s],
            send_sem=gather_send,
            recv_sem=gather_recv.at[step, s],
            device_id={"etp": ahead},
            device_id_type=MESH,
        )

    def arrival(step, s):
        chunk = lax.rem(chip - way * (step + 1) + 2 * RING, RING)
        return pltpu.make_async_remote_copy(
            src_ref=tiles.at[chunk, s],
            dst_ref=tiles.at[chunk, s],
            send_sem=gather_send,
            recv_sem=gather_recv.at[step, s],
            device_id={"etp": ahead},
            device_id_type=MESH,
        )

    def sib_copy(step, s):
        chunk = lax.rem(chip - way * step + 2 * RING, RING)
        return pltpu.make_async_remote_copy(
            src_ref=tiles.at[chunk, s],
            dst_ref=sib_tiles.at[chunk, s],
            send_sem=sib_send,
            recv_sem=sib_recv.at[step, s],
            device_id={"etp": sibling},
            device_id_type=MESH,
        )

    def sib_arrival(step, s):
        chunk = lax.rem(chip + way * step + 2 * RING, RING)
        return pltpu.make_async_remote_copy(
            src_ref=tiles.at[chunk, s],
            dst_ref=sib_tiles.at[chunk, s],
            send_sem=sib_send,
            recv_sem=sib_recv.at[step, s],
            device_id={"etp": sibling},
            device_id_type=MESH,
        )

    def expand(store, chunk, of_core, s):
        row, column = place(chunk, of_core, s)
        tile = store[chunk, s]
        for target, part in zip((w_high, w_mid, w_low), split(tile)):
            target[row, column] = part
        for target, part in zip((w_high, w_mid, w_low), split(tile.T)):
            target[column, row] = part

    own_tiles(chip)
    for s in range(TILES):
        ring_copy(RING - 2, s).wait_recv()
        tiles[chip, s] = mine[s] + ring_in[RING - 2, s]
        gather_copy(0, s).start()
        sib_copy(0, s).start()

    @pl.loop(0, RING)
    def _(step):
        chunk = lax.rem(chip - way * step + 2 * RING, RING)
        sib_chunk = lax.rem(chip + way * step + 2 * RING, RING)
        for s in range(TILES):
            expand(tiles, chunk, core, s)
        for s in range(TILES):
            sib_arrival(step, s).wait_recv()
            expand(sib_tiles, sib_chunk, 1 - core, s)

        @pl.when(step < RING - 1)
        def _():
            for s in range(TILES):
                arrival(step, s).wait_recv()
                sib_copy(step + 1, s).start()

        @pl.when(step < RING - 2)
        def _():
            for s in range(TILES):
                gather_copy(step + 1, s).start()

    def through_gram(values, target):
        high, middle, low = split(values)
        three = jnp.concatenate([high, middle, low], axis=0)
        two = jnp.concatenate([high, middle], axis=0)
        for n in range(BLOCKS // 2):
            def wide_block(store):
                return jnp.concatenate(
                    [
                        jnp.concatenate([store[i, 2 * n], store[i, 2 * n + 1]], axis=1)
                        for i in range(BLOCKS)
                    ],
                    axis=0,
                )
            first = nn(three, wide_block(w_high))
            second = nn(two, wide_block(w_mid))
            third = nn(high, wide_block(w_low))
            result = first[:RANK] + (
                (first[RANK : 2 * RANK] + second[:RANK])
                + ((first[2 * RANK :] + second[RANK:]) + third)
            )
            target[:, 2 * BLOCK * n : 2 * BLOCK * (n + 1)] = result

    def gram_of(former, latter):
        both = nt(
            jnp.concatenate(split(former), axis=0), jnp.concatenate(split(latter), axis=0)
        )
        part = lambda i, j: both[RANK * i : RANK * (i + 1), RANK * j : RANK * (j + 1)]
        return part(0, 0) + (
            (part(0, 1) + part(1, 0)) + (part(1, 1) + (part(0, 2) + part(2, 0)))
        )

    r_ref[...] = q_ref[...].T

    def normalise(inverse):
        a_ref[...] = nn(inverse, z_ref[...], HIGHEST)
        across = a_ref[...]
        norm = jnp.sum(across * across, axis=1, keepdims=True) + epsilon
        return across, lax.rsqrt(norm)

    @pl.loop(0, DIRECT)
    def _(turn):
        through_gram(r_ref[...], z_ref)
        inverse = inverse_cholesky(gram_of(r_ref[...], z_ref[...]))
        across, scale = normalise(inverse)
        r_ref[...] = across * scale

    through_gram(r_ref[...], z_ref)

    @pl.loop(DIRECT, ITERS - 1)
    def _(turn):
        through_gram(z_ref[...], v_ref)
        inverse = inverse_cholesky(gram_of(r_ref[...], z_ref[...]))
        across, scale = normalise(inverse)
        r_ref[...] = across * scale
        z_ref[...] = nn(inverse * scale, v_ref[...], HIGHEST)

    inverse = inverse_cholesky(gram_of(r_ref[...], z_ref[...]))
    s_out[...] = nn(inverse, r_ref[...], HIGHEST)
    across, scale = normalise(inverse)
    a_out[...] = across
    r_out[...] = across * scale

    for copies_of, store in ((ring_send, ring_out), (gather_send, tiles)):
        sent = store.at[pl.ds(0, RING - 1)]
        pltpu.make_async_copy(sent, sent, copies_of).wait()
    pltpu.make_async_copy(tiles, tiles, sib_send).wait()


def finish_kernel(m_ref, g_ref, clip_ref, s_ref, a_ref, r_ref, m_out, q_out, u_out):
    clip = clip_ref[0:1, 0:1]
    blended = m_ref[...] + clip * g_ref[...].astype(F32)
    left = nt(blended, s_ref[...], HIGHEST)
    m_out[...] = blended - (1.0 - keep_rate) * nn(left, a_ref[...], HIGHEST)
    update_scale = math.sqrt(ROWS * COLS / RANK)
    u_out[...] = (update_scale * nn(left, r_ref[...], HIGHEST)).astype(BF16)
    q_out[...] = r_ref[...].T


def body(momentum, grad, q_in):
    dp_size = lax.axis_size("dp")
    rows, cols = momentum.shape[1:]
    element_count = float(dp_size * rows * 2 * RING * cols)
    m, g, q = momentum[0], grad[0], q_in[0]
    vmem = pl.BlockSpec(memory_space=pltpu.VMEM)
    tile = (BLOCK, BLOCK)
    s_t, a_t, r_t, clip = pl.pallas_call(
        functools.partial(refresh_kernel, dp_size, element_count),
        out_shape=[jax.ShapeDtypeStruct((RANK, cols), F32)] * 3
        + [jax.ShapeDtypeStruct((8, BLOCK), F32)],
        in_specs=[vmem] * 3,
        out_specs=[vmem] * 4,
        scratch_shapes=[
            pltpu.VMEM((rows, cols), F32),
            pltpu.VMEM((rows, cols), F32),
            pltpu.VMEM((rows, cols), F32),
            pltpu.VMEM((2 * RING, 8, BLOCK), F32),
            pltpu.VMEM((dp_size, 8, BLOCK), F32),
            pltpu.VMEM((BLOCKS, 2 * rows, 3 * BLOCK), BF16),
            pltpu.VMEM((BLOCKS, 3 * BLOCK, 2 * rows), BF16),
            pltpu.VMEM((TILES,) + tile, F32),
            pltpu.VMEM((RING - 1, TILES) + tile, F32),
            pltpu.VMEM((RING - 1, TILES) + tile, F32),
            pltpu.VMEM((RING, TILES) + tile, F32),
            pltpu.VMEM((RING, TILES) + tile, F32),
            pltpu.VMEM((BLOCKS, BLOCKS) + tile, BF16),
            pltpu.VMEM((BLOCKS, BLOCKS) + tile, BF16),
            pltpu.VMEM((BLOCKS, BLOCKS) + tile, BF16),
            pltpu.VMEM((RANK, cols), F32),
            pltpu.VMEM((RANK, cols), F32),
            pltpu.VMEM((RANK, cols), F32),
            pltpu.VMEM((RANK, cols), F32),
            pltpu.SemaphoreType.DMA((2,)),
            pltpu.SemaphoreType.DMA((2,)),
            pltpu.SemaphoreType.DMA((2,)),
            pltpu.SemaphoreType.DMA((2,)),
            pltpu.SemaphoreType.DMA,
            pltpu.SemaphoreType.DMA((RING - 1, TILES)),
            pltpu.SemaphoreType.DMA,
            pltpu.SemaphoreType.DMA((RING - 1, TILES)),
            pltpu.SemaphoreType.DMA,
            pltpu.SemaphoreType.DMA((RING, TILES)),
        ],
        compiler_params=pltpu.CompilerParams(
            collective_id=0, has_side_effects=True, vmem_limit_bytes=58 << 20
        ),
    )(m, g, q)
    part = rows // 2
    whole = lambda shape: pl.BlockSpec(shape, lambda n: (0, 0))
    by_rows = pl.BlockSpec((part, cols), lambda n: (n, 0))
    m_new, q_new, update = pl.pallas_call(
        finish_kernel,
        grid=(2,),
        out_shape=[
            jax.ShapeDtypeStruct((rows, cols), F32),
            jax.ShapeDtypeStruct((cols, RANK), F32),
            jax.ShapeDtypeStruct((rows, cols), BF16),
        ],
        in_specs=[by_rows, by_rows, whole((8, BLOCK))] + [whole((RANK, cols))] * 3,
        out_specs=[by_rows, whole((cols, RANK)), by_rows],
        compiler_params=pltpu.CompilerParams(vmem_limit_bytes=58 << 20),
    )(m, g, clip, s_t, a_t, r_t)
    return m_new[None], q_new[None], update[None]


def solution(mesh):
    return jax.shard_map(
        body,
        mesh=mesh,
        in_specs=(P("dp", "etp", None), P("dp", "etp", None), P("dp", None, None)),
        out_specs=(P("dp", "etp", None), P("dp", None, None), P("dp", "etp", None)),
        check_vma=False,
    )
```

time: 1570 us -> 166 us (0.11)
  waiting for transfers between devices: 927 us -> 0 us
  blocking collectives: 469 us -> 0 us
  Pallas kernels: 0 us -> 161 us
  other arithmetic: 111 us -> 0 us
  matrix products: 41 us -> 0 us
    psum x8 -> x0, waiting for transfers between devices: 927 us -> none  [body(): across = lax.psum(product('erc,erk->eck', blended, left_basis), 'etp')]
    psum x9 -> x0, blocking collectives: 469 us -> none  [the longest x8 363 us: body(): gram_matrix = lax.psum(product('erk,erl->ekl', raw_left, raw_left), 'etp')]
    pallas_call x0 -> x2, Pallas kernels: none -> 161 us  [the longest x1 153 us: body(): pl.pallas_call(functools.partial(refresh_kernel, dp_size, element_count),...]
    another operation x40 -> x0, other arithmetic: 96.5 us -> none  [the longest x24 52.2 us: body(): lower_factor = jnp.linalg.cholesky(gram_matrix)]
    dot_general x26 -> x0, matrix products: 38.9 us -> none  [product(): jnp.einsum(pattern, former, latter, precision=lax.Precision.HIGHEST, pref...]
  transfers between devices with their start and end apart: 8 -> 0, of which waited for: 8 -> 0; matrix products, arithmetic and copies ran while one was open for 0% -> 0% of each run, Pallas kernels for 0% -> 0%
where the time goes in v1:
time: 166 us
  Pallas kernels  161 us (97%)
  local copies, waits for them, and re-layouts  4.28 us (3%)
    pallas_call x1, Pallas kernels, body(): pl.pallas_call(functools.partial(refresh_kernel, dp_size, element_count),...  153 us
    pallas_call x1, Pallas kernels, body(): pl.pallas_call(finish_kernel, grid=(2,), out_shape=[jax.ShapeDtypeStruct(...  8.44 us
    unnamed x2, local copies, waits for them, and re-layouts  4.28 us

profile of v1, /device:TPU:1, one launch (start us, length us, event | category | flops | bytes accessed | tf_op | source)
XLA Modules:
  0.0 166.1 jit_solution(14226750219981514117)
XLA Ops:
  0.6 2.1 %copy.6 = f32[1,1536,64]{2,1,0:T(8,128)} copy(f32[1,1536,64]{1,2,0:T(8,128)} %param.5) | data formatting | bytes 786432 | tf_op args[2]
  2.8 152.7 %shard_map.58 = (f32[64,1536]{1,0:T(8,128)}, f32[64,1536]{1,0:T(8,128)}, f32[64,1536]{1,0:T(8,128)}, f32[8,128]{1,0:T(8,128)}) custom-call(f32[224,1536]{1,0:T(8,128)} %bitcast.6, bf16[224,1536]{1,0:T(8,128)(2,1)} %bitcast.9, f32[1536,64]{1,0:T(8,128)} %bitcast.8), custom_call_target="tpu_custom_call" | custom-call | tf_op jit(solution)/shard_map/pallas_call | solution.py:438
  155.5 8.4 %shard_map.59 = (f32[224,1536]{1,0:T(8,128)}, f32[1536,64]{1,0:T(8,128)}, bf16[224,1536]{1,0:T(8,128)(2,1)}) custom-call(f32[224,1536]{1,0:T(8,128)} %bitcast.7, bf16[224,1536]{1,0:T(8,128)(2,1)} %bitcast.10, f32[8,128]{1,0:T(8,128)} %get-tuple-element.10.clip_ref, f32[64,1536]{1,0:T(8,128)} %get-tuple-element.11.s_ref, f32[64,1536]{1,0:T(8,128)} %get-tuple-element.12.a_ref, ...), custom_call_target="tpu_custom_call" | custom-call | tf_op jit(solution)/shard_map/pallas_call | solution.py:482
  163.9 2.1 %copy.7 = f32[1,1536,64]{1,2,0:T(8,128)} copy(f32[1,1536,64]{2,1,0:T(8,128)} %bitcast.11) | data formatting | bytes 786432

commit v2 on v1

v2 whole, which is shorter than its diff:
```python
import functools
import math

import jax
import jax.numpy as jnp
from jax import lax
from jax.experimental import pallas as pl
from jax.experimental.pallas import tpu as pltpu
from jax.sharding import PartitionSpec as P

ROWS = 3584
COLS = 1536
RANK = 64
ITERS = 8
DIRECT = 3

BLOCK = 128
BLOCKS = COLS // BLOCK
TILES = 5
HALVES = 2
RING = 8
LONG = RING // 2
SHORT = RING - 1 - LONG

keep_rate = 0.9
epsilon = 1e-06

MESH = pl.DeviceIdType.MESH
F32 = jnp.float32
BF16 = jnp.bfloat16


def nn(former, latter):
    return jnp.dot(former, latter, preferred_element_type=F32)


def nt(former, latter):
    return lax.dot_general(former, latter, (((1,), (1,)), ((), ())), preferred_element_type=F32)


def split(values, terms):
    parts = []
    for _ in range(terms):
        parts.append(values.astype(BF16))
        values = values - parts[-1].astype(F32)
    return parts


def inverse_cholesky(gram, between=()):
    full = (8, 2 * RANK)
    ones = lax.broadcasted_iota(jnp.int32, (RANK, RANK), 0) == lax.broadcasted_iota(
        jnp.int32, (RANK, RANK), 1
    )
    joined = jnp.concatenate([gram, ones.astype(F32)], axis=1)
    panels = [joined[8 * p : 8 * p + 8] for p in range(RANK // 8)]
    sublane = lax.broadcasted_iota(jnp.int32, full, 0)
    for p in range(RANK // 8):
        if p < len(between):
            between[p]()
        panel = panels[p]
        entry = [[None] * 8 for _ in range(8)]
        for i in range(8):
            for j in range(i + 1):
                entry[i][j] = jnp.broadcast_to(panel[i : i + 1, 8 * p + j : 8 * p + j + 1], full)
        rows = [jnp.broadcast_to(panel[i : i + 1, :], full) for i in range(8)]
        scale = [None] * 8
        factor = [[None] * 8 for _ in range(8)]
        for j in range(8):
            scale[j] = lax.rsqrt(entry[j][j])
            for i in range(j + 1, 8):
                factor[i][j] = entry[i][j] * scale[j]
            for i in range(j + 1, 8):
                for m in range(j + 1, i + 1):
                    entry[i][m] = entry[i][m] - factor[i][j] * factor[m][j]
            rows[j] = rows[j] * scale[j]
            for i in range(j + 1, 8):
                rows[i] = rows[i] - factor[i][j] * rows[j]
        done = rows[0]
        for i in range(1, 8):
            done = jnp.where(sublane == i, rows[i], done)
        panels[p] = done
        for q in range(p + 1, RANK // 8):
            column = [
                jnp.broadcast_to(panels[q][:, 8 * p + j : 8 * p + j + 1], full) for j in range(8)
            ]
            for j in range(8):
                column[j] = column[j] * scale[j]
                for i in range(j + 1, 8):
                    column[i] = column[i] - factor[i][j] * column[j]
            left = panels[q]
            for j in range(8):
                left = left - column[j] * rows[j]
            panels[q] = left
    return jnp.concatenate(panels, axis=0)[:, RANK:]


def refresh_kernel(
    dp_size,
    element_count,
    m_hbm,
    g_hbm,
    q_hbm,
    left_out,
    r_out,
    clip_out,
    m_ref,
    g_ref,
    q_ref,
    wide,
    other_m,
    other_g,
    sums,
    totals,
    tall,
    flat,
    own_far,
    own_near,
    far_in,
    far_out,
    near_in,
    near_out,
    tiles,
    sib_tiles,
    w_high,
    w_mid,
    r_terms,
    z_terms,
    v_terms,
    v_ref,
    load,
    small_send,
    small_recv,
    big_send,
    big_recv,
    ring_send,
    far_recv,
    near_recv,
    gather_send,
    gather_far_recv,
    gather_near_recv,
    sib_send,
    sib_recv,
):
    me = lax.axis_index("etp")
    dp = lax.axis_index("dp")
    etp_size = 2 * RING
    chip = me // 2
    core = lax.rem(me, 2)
    sibling = chip * 2 + (1 - core)
    way = 1 - 2 * core
    ahead = lax.rem(chip + way + RING, RING) * 2 + core
    behind = lax.rem(chip - way + RING, RING) * 2 + core
    rows = m_ref.shape[0]

    barrier = pltpu.get_barrier_semaphore()

    @pl.loop(1, etp_size)
    def _(step):
        pl.semaphore_signal(
            barrier, inc=1, device_id={"etp": lax.rem(me + step, etp_size)}, device_id_type=MESH
        )

    @pl.loop(1, dp_size)
    def _(step):
        pl.semaphore_signal(
            barrier, inc=1, device_id={"dp": lax.rem(dp + step, dp_size)}, device_id_type=MESH
        )

    loads = [
        pltpu.make_async_copy(source, target, load.at[n])
        for n, (source, target) in enumerate(((g_hbm, g_ref), (m_hbm, m_ref), (q_hbm, q_ref)))
    ]
    for copy in loads:
        copy.start()
    loads[0].wait()
    wide[...] = g_ref[...].astype(F32)
    partial = jnp.zeros((8, BLOCK), F32)
    for b in range(BLOCKS):
        piece = wide[:, BLOCK * b : BLOCK * (b + 1)]
        partial = partial + jnp.sum((piece * piece).reshape(rows // 8, 8, BLOCK), axis=0)
    sums[me] = partial
    loads[1].wait()
    loads[2].wait()

    pl.semaphore_wait(barrier, etp_size + dp_size - 2)

    @pl.loop(1, etp_size)
    def _(step):
        pltpu.make_async_remote_copy(
            src_ref=sums.at[me],
            dst_ref=sums.at[me],
            send_sem=small_send.at[0],
            recv_sem=small_recv.at[0],
            device_id={"etp": lax.rem(me + step, etp_size)},
            device_id_type=MESH,
        ).start()

    copies = [
        pltpu.make_async_remote_copy(
            src_ref=source,
            dst_ref=target,
            send_sem=big_send.at[n],
            recv_sem=big_recv.at[n],
            device_id={"etp": sibling},
            device_id_type=MESH,
        )
        for n, (source, target) in enumerate(((m_ref, other_m), (wide, other_g)))
    ]
    for copy in copies:
        copy.start()

    others = sums.at[pl.ds(0, etp_size - 1)]
    pltpu.make_async_copy(others, others, small_recv.at[0]).wait()
    group = sums[0]
    for n in range(1, etp_size):
        group = group + sums[n]
    totals[dp] = group

    if dp_size > 1:

        @pl.loop(1, dp_size)
        def _(step):
            pltpu.make_async_remote_copy(
                src_ref=totals.at[dp],
                dst_ref=totals.at[dp],
                send_sem=small_send.at[1],
                recv_sem=small_recv.at[1],
                device_id={"dp": lax.rem(dp + step, dp_size)},
                device_id_type=MESH,
            ).start()

        far = totals.at[pl.ds(0, dp_size - 1)]
        pltpu.make_async_copy(far, far, small_recv.at[1]).wait()
        pltpu.make_async_copy(far, far, small_send.at[1]).wait()
    pltpu.make_async_copy(others, others, small_send.at[0]).wait()
    everything = totals[0]
    for n in range(1, dp_size):
        everything = everything + totals[n]
    total_sq = jnp.sum(jnp.sum(everything, axis=0, keepdims=True), axis=1, keepdims=True)
    clip = jnp.minimum(1.0, lax.rsqrt(total_sq / element_count + epsilon))
    clip_out[...] = jnp.broadcast_to(clip, (8, BLOCK))
    for copy in copies:
        copy.wait()

    for b in range(BLOCKS):
        columns = slice(BLOCK * b, BLOCK * (b + 1))
        own = m_ref[:, columns] + clip * wide[:, columns]
        sib = other_m[:, columns] + clip * other_g[:, columns]
        blended = jnp.concatenate([own, sib], axis=0)
        for n, part in enumerate(split(blended, 2)):
            tall[b, :, BLOCK * n : BLOCK * (n + 1)] = part
        for n, part in enumerate(split(blended.T, 2)):
            flat[b, BLOCK * n : BLOCK * (n + 1), :] = part

    def place(chunk, of_core, s):
        tile = TILES * (2 * chunk + of_core) + s
        row = lax.rem(tile, BLOCKS)
        return row, lax.rem(row + tile // BLOCKS, BLOCKS)

    def own_tile(store, chunk, s):
        row, column = place(chunk, core, s)
        both = nn(flat[row], tall[column])
        part = lambda i, j: both[BLOCK * i : BLOCK * (i + 1), BLOCK * j : BLOCK * (j + 1)]
        store[s] = part(0, 0) + (part(0, 1) + (part(1, 0) + part(1, 1)))

    def at(steps):
        return lax.rem(chip + way * steps + RING, RING)

    half = BLOCK // HALVES
    halves = [(h, pl.ds(half * h, half)) for h in range(HALVES)]

    def remote(source, target, send, recv, device):
        return pltpu.make_async_remote_copy(
            src_ref=source,
            dst_ref=target,
            send_sem=send,
            recv_sem=recv,
            device_id={"etp": device},
            device_id_type=MESH,
        )

    def far_copy(step, s, h, rows):
        return remote(
            far_out.at[step, s, rows],
            far_in.at[step, s, rows],
            ring_send.at[0],
            far_recv.at[step, s, h],
            ahead,
        )

    def near_copy(step, s, h, rows):
        return remote(
            near_out.at[step, s, rows],
            near_in.at[step, s, rows],
            ring_send.at[1],
            near_recv.at[step, s, h],
            behind,
        )

    def gather_far(step, chunk, s, h, rows):
        place_of = tiles.at[chunk, s, rows]
        return remote(
            place_of, place_of, gather_send.at[0], gather_far_recv.at[step, s, h], ahead
        )

    def gather_near(step, chunk, s, h, rows):
        place_of = tiles.at[chunk, s, rows]
        return remote(
            place_of, place_of, gather_send.at[1], gather_near_recv.at[step, s, h], behind
        )

    def sib_copy(order, chunk, s, h, rows):
        return remote(
            tiles.at[chunk, s, rows],
            sib_tiles.at[chunk, s, rows],
            sib_send,
            sib_recv.at[order, s, h],
            sibling,
        )

    def expand(store, chunk, of_core, s):
        row, column = place(chunk, of_core, s)
        tile = store[chunk, s]
        for target, part in zip((w_high, w_mid), split(tile, 2)):
            target[row, column] = part
        for target, part in zip((w_high, w_mid), split(tile.T, 2)):
            target[column, row] = part

    def sib_expand(order, s):
        steps = 0 if order == 0 else (order + 1) // 2 if order % 2 else -(order // 2)
        for h, rows in halves:
            sib_copy(order, at(steps), s, h, rows).wait_recv()
        expand(sib_tiles, at(steps), 1 - core, s)

    @pl.loop(0, TILES)
    def _(s):
        own_tile(own_far, at(LONG), s)
        for h, rows in halves:
            far_out[0, s, rows] = own_far[s, rows]
            far_copy(0, s, h, rows).start()
        own_tile(own_near, at(-SHORT), s)
        for h, rows in halves:
            near_out[0, s, rows] = own_near[s, rows]
            near_copy(0, s, h, rows).start()

    @pl.loop(0, TILES)
    def _(s):
        own_tile(own_far, at(LONG - 1), s)
        own_tile(own_near, at(1 - SHORT), s)

    for step in range(1, LONG):

        @pl.loop(0, TILES)
        def _(s):
            for h, rows in halves:
                far_copy(step - 1, s, h, rows).wait_recv()
                far_out[step, s, rows] = own_far[s, rows] + far_in[step - 1, s, rows]
                far_copy(step, s, h, rows).start()
            own_tile(own_far, at(LONG - 1 - step), s)
            if step < SHORT:
                for h, rows in halves:
                    near_copy(step - 1, s, h, rows).wait_recv()
                    near_out[step, s, rows] = own_near[s, rows] + near_in[step - 1, s, rows]
                    near_copy(step, s, h, rows).start()
                if step < SHORT - 1:
                    own_tile(own_near, at(step + 1 - SHORT), s)

    @pl.loop(0, TILES)
    def _(s):
        for h, rows in halves:
            near_copy(SHORT - 1, s, h, rows).wait_recv()
            far_copy(LONG - 1, s, h, rows).wait_recv()
            tiles[chip, s, rows] = (
                own_far[s, rows] + near_in[SHORT - 1, s, rows] + far_in[LONG - 1, s, rows]
            )
            gather_far(0, chip, s, h, rows).start()
            gather_near(0, chip, s, h, rows).start()
            sib_copy(0, chip, s, h, rows).start()
        expand(tiles, chip, core, s)

    for step in range(LONG):

        @pl.loop(0, TILES)
        def _(s):
            from_behind, from_ahead = at(-1 - step), at(1 + step)
            for h, rows in halves:
                gather_far(step, from_behind, s, h, rows).wait_recv()
                if step < LONG - 1:
                    gather_far(step + 1, from_behind, s, h, rows).start()
                sib_copy(2 * step + 1, from_behind, s, h, rows).start()
            expand(tiles, from_behind, core, s)
            if step < SHORT:
                for h, rows in halves:
                    gather_near(step, from_ahead, s, h, rows).wait_recv()
                    if step < SHORT - 1:
                        gather_near(step + 1, from_ahead, s, h, rows).start()
                    sib_copy(2 * step + 2, from_ahead, s, h, rows).start()
                expand(tiles, from_ahead, core, s)
            for order in range(max(0, 2 * step - 1), 2 * step + 1):
                sib_expand(order, s)

    @pl.loop(0, TILES)
    def _(s):
        sib_expand(RING - 1, s)

    def keep(values, target):
        for n, part in enumerate(split(values, 3)):
            target[RANK * n : RANK * (n + 1), :] = part

    def gram_columns(terms, n):
        def weights(store):
            return jnp.concatenate(
                [
                    jnp.concatenate([store[i, 2 * n], store[i, 2 * n + 1]], axis=1)
                    for i in range(BLOCKS)
                ],
                axis=0,
            )

        first = nn(terms[...], weights(w_high))
        second = nn(terms[: 2 * RANK, :], weights(w_mid))
        v_ref[:, 2 * BLOCK * n : 2 * BLOCK * (n + 1)] = first[:RANK] + (
            (first[RANK : 2 * RANK] + second[:RANK]) + (first[2 * RANK :] + second[RANK:])
        )

    def small_gram():
        both = nt(r_terms[...], z_terms[...])
        part = lambda i, j: both[RANK * i : RANK * (i + 1), RANK * j : RANK * (j + 1)]
        return part(0, 0) + (
            (part(0, 1) + part(1, 0)) + (part(1, 1) + (part(0, 2) + part(2, 0)))
        )

    def apply(inverse, terms):
        high, middle, low = split(inverse, 3)
        none = jnp.zeros_like(high)
        stack = jnp.concatenate(
            [
                jnp.concatenate([high, high, high], axis=1),
                jnp.concatenate([middle, middle, none], axis=1),
                jnp.concatenate([low, none, none], axis=1),
            ],
            axis=0,
        )
        result = nn(stack, terms[...])
        return result[:RANK] + (result[RANK : 2 * RANK] + result[2 * RANK :])

    def normalise(across):
        return lax.rsqrt(jnp.sum(across * across, axis=1, keepdims=True) + epsilon)

    keep(q_ref[...], r_terms)

    @pl.loop(0, DIRECT)
    def _(turn):
        for n in range(BLOCKS // 2):
            gram_columns(r_terms, n)
        keep(v_ref[...], z_terms)
        inverse = inverse_cholesky(small_gram())
        across = apply(inverse, z_terms)
        keep(across * normalise(across), r_terms)

    for n in range(BLOCKS // 2):
        gram_columns(r_terms, n)
    keep(v_ref[...], z_terms)

    @pl.loop(DIRECT, ITERS - 1)
    def _(turn):
        inverse = inverse_cholesky(
            small_gram(),
            [functools.partial(gram_columns, z_terms, n) for n in range(BLOCKS // 2)],
        )
        keep(v_ref[...], v_terms)
        across = apply(inverse, z_terms)
        ahead_of = apply(inverse, v_terms)
        scale = normalise(across)
        keep(across * scale, r_terms)
        keep(ahead_of * scale, z_terms)

    inverse = inverse_cholesky(small_gram())
    across = apply(inverse, z_terms)
    scale = normalise(across)
    r_out[...] = across * scale
    left_map = apply(inverse, r_terms)
    norm = scale * (jnp.sum(across * across, axis=1, keepdims=True) + epsilon)
    maps = jnp.concatenate(split(left_map * norm, 2) + split(left_map, 2), axis=0)
    blended = m_ref[...] + clip * wide[...]
    both = nt(jnp.concatenate(split(blended, 2), axis=0), maps)
    both = both[:rows] + both[rows:]
    for n in range(2):
        first = both[:, 2 * RANK * n : 2 * RANK * n + RANK]
        left_out[:, RANK * n : RANK * (n + 1)] = (
            first + both[:, 2 * RANK * n + RANK : 2 * RANK * (n + 1)]
        )

    for sent, semaphore in (
        (far_out, ring_send.at[0]),
        (near_out, ring_send.at[1]),
        (tiles.at[pl.ds(0, LONG)], gather_send.at[0]),
        (tiles.at[pl.ds(0, SHORT)], gather_send.at[1]),
        (tiles, sib_send),
    ):
        pltpu.make_async_copy(sent, sent, semaphore).wait()


def finish_kernel(m_ref, g_ref, clip_ref, left_ref, r_ref, m_out, q_out, u_out):
    blended = m_ref[...] + clip_ref[0:1, 0:1] * g_ref[...].astype(F32)
    rows = blended.shape[0]
    left = jnp.concatenate([left_ref[:, :RANK], left_ref[:, RANK:]], axis=0)
    high, middle = split(left, 2)
    right = split(r_ref[...], 2)
    outer = nn(
        jnp.concatenate([high, high, middle, middle], axis=1),
        jnp.concatenate(right + right, axis=0),
    )
    m_out[...] = blended - (1.0 - keep_rate) * outer[:rows]
    update_scale = math.sqrt(ROWS * COLS / RANK)
    u_out[...] = (update_scale * outer[rows:]).astype(BF16)
    q_out[...] = r_ref[...]


def body(momentum, grad, q_in):
    dp_size = lax.axis_size("dp")
    rows, cols = momentum.shape[1:]
    element_count = float(dp_size * rows * 2 * RING * cols)
    m, g, q = momentum[0], grad[0], q_in[0].T
    vmem = pl.BlockSpec(memory_space=pltpu.VMEM)
    hbm = pl.BlockSpec(memory_space=pl.ANY)
    tile = (BLOCK, BLOCK)
    dma = pltpu.SemaphoreType.DMA
    left, r_t, clip = pl.pallas_call(
        functools.partial(refresh_kernel, dp_size, element_count),
        out_shape=[
            jax.ShapeDtypeStruct((rows, 2 * RANK), F32),
            jax.ShapeDtypeStruct((RANK, cols), F32),
            jax.ShapeDtypeStruct((8, BLOCK), F32),
        ],
        in_specs=[hbm] * 3,
        out_specs=[vmem] * 3,
        scratch_shapes=[
            pltpu.VMEM((rows, cols), F32),
            pltpu.VMEM((rows, cols), BF16),
            pltpu.VMEM((RANK, cols), F32),
            pltpu.VMEM((rows, cols), F32),
            pltpu.VMEM((rows, cols), F32),
            pltpu.VMEM((rows, cols), F32),
            pltpu.VMEM((2 * RING, 8, BLOCK), F32),
            pltpu.VMEM((dp_size, 8, BLOCK), F32),
            pltpu.VMEM((BLOCKS, 2 * rows, 2 * BLOCK), BF16),
            pltpu.VMEM((BLOCKS, 2 * BLOCK, 2 * rows), BF16),
            pltpu.VMEM((TILES,) + tile, F32),
            pltpu.VMEM((TILES,) + tile, F32),
            pltpu.VMEM((LONG, TILES) + tile, F32),
            pltpu.VMEM((LONG, TILES) + tile, F32),
            pltpu.VMEM((SHORT, TILES) + tile, F32),
            pltpu.VMEM((SHORT, TILES) + tile, F32),
            pltpu.VMEM((RING, TILES) + tile, F32),
            pltpu.VMEM((RING, TILES) + tile, F32),
            pltpu.VMEM((BLOCKS, BLOCKS) + tile, BF16),
            pltpu.VMEM((BLOCKS, BLOCKS) + tile, BF16),
            pltpu.VMEM((3 * RANK, cols), BF16),
            pltpu.VMEM((3 * RANK, cols), BF16),
            pltpu.VMEM((3 * RANK, cols), BF16),
            pltpu.VMEM((RANK, cols), F32),
            dma((3,)),
            dma((2,)),
            dma((2,)),
            dma((2,)),
            dma((2,)),
            dma((2,)),
            dma((LONG, TILES, HALVES)),
            dma((SHORT, TILES, HALVES)),
            dma((2,)),
            dma((LONG, TILES, HALVES)),
            dma((SHORT, TILES, HALVES)),
            dma,
            dma((RING, TILES, HALVES)),
        ],
        compiler_params=pltpu.CompilerParams(
            collective_id=0, has_side_effects=True, vmem_limit_bytes=56 << 20
        ),
    )(m, g, q)
    part = rows // 2
    whole = lambda shape: pl.BlockSpec(shape, lambda n: (0, 0))
    by_rows = pl.BlockSpec((part, cols), lambda n: (n, 0))
    m_new, q_new, update = pl.pallas_call(
        finish_kernel,
        grid=(2,),
        out_shape=[
            jax.ShapeDtypeStruct((rows, cols), F32),
            jax.ShapeDtypeStruct((RANK, cols), F32),
            jax.ShapeDtypeStruct((rows, cols), BF16),
        ],
        in_specs=[
            by_rows,
            by_rows,
            whole((8, BLOCK)),
            pl.BlockSpec((part, 2 * RANK), lambda n: (n, 0)),
            whole((RANK, cols)),
        ],
        out_specs=[by_rows, whole((RANK, cols)), by_rows],
        compiler_params=pltpu.CompilerParams(vmem_limit_bytes=24 << 20),
    )(m, g, clip, left, r_t)
    return m_new[None], q_new.T[None], update[None]


def solution(mesh):
    return jax.shard_map(
        body,
        mesh=mesh,
        in_specs=(P("dp", "etp", None), P("dp", "etp", None), P("dp", None, None)),
        out_specs=(P("dp", "etp", None), P("dp", None, None), P("dp", "etp", None)),
        check_vma=False,
    )
```

time: 166 us -> 123 us (0.74)
  Pallas kernels: 161 us -> 119 us
  local copies, waits for them, and re-layouts: 4.28 us -> 2.56 us
    pallas_call x1, Pallas kernels: 153 us -> 117 us  [body(): pl.pallas_call(functools.partial(refresh_kernel, dp_size, element_count),...]
    pallas_call x1, Pallas kernels: 8.44 us -> 1.94 us  [body(): pl.pallas_call(finish_kernel, grid=(2,), out_shape=[jax.ShapeDtypeStruct(...]
    unnamed x2 -> x10, local copies, waits for them, and re-layouts: 4.28 us -> 2.56 us
where the time goes in v2:
time: 123 us
  Pallas kernels  119 us (97%)
  local copies, waits for them, and re-layouts  2.56 us (2%)
    pallas_call x1, Pallas kernels, body(): pl.pallas_call(functools.partial(refresh_kernel, dp_size, element_count),...  117 us
    unnamed x10, local copies, waits for them, and re-layouts  2.56 us

profile of v2, /device:TPU:1, one launch (start us, length us, event | category | flops | bytes accessed | tf_op | source)
XLA Modules:
  0.0 122.6 jit_solution(11848765551087188401)
XLA Ops:
  0.6 0.0 copy-start.1
  0.6 0.0 copy-start
  0.7 117.4 %shard_map.58 = (f32[224,128]{1,0:T(8,128)}, f32[64,1536]{1,0:T(8,128)}, f32[8,128]{1,0:T(8,128)}) custom-call(f32[224,1536]{1,0:T(8,128)} %bitcast.10, bf16[224,1536]{1,0:T(8,128)(2,1)} %bitcast.12, f32[64,1536]{1,0:T(8,128)} %bitcast.14), custom_call_target="tpu_custom_call" | custom-call | tf_op jit(solution)/shard_map/pallas_call | solution.py:529
  118.1 0.0 copy-done.1
  118.1 0.0 copy-done
  118.1 0.0 copy-start.2
  118.1 1.0 copy-done.2
  119.1 0.0 copy-start.3
  119.1 0.9 copy-done.3
  120.0 0.0 copy-start.4
  120.0 0.7 copy-done.4
  120.7 1.9 %shard_map.59 = (f32[224,1536]{1,0:T(8,128)}, f32[64,1536]{1,0:T(8,128)}, bf16[224,1536]{1,0:T(8,128)(2,1)}) custom-call(f32[224,1536]{1,0:T(8,128)S(1)} %bitcast.11, bf16[224,1536]{1,0:T(8,128)(2,1)S(1)} %bitcast.13, f32[8,128]{1,0:T(8,128)S(1)} %copy-done.4, f32[224,128]{1,0:T(8,128)S(1)} %copy-done.3, f32[64,1536]{1,0:T(8,128)S(1)} %copy-done.2), custom_call_target="tpu_custom_call" | custom-call | tf_op jit(solution)/shard_map/pallas_call | solution.py:584
Async XLA Ops:
  0.6 117.5 %copy-start.1 = (bf16[1,224,1536]{2,1,0:T(8,128)(2,1)S(1)}, bf16[1,224,1536]{2,1,0:T(8,128)(2,1)}, u32[]{:S(2)}) copy-start(bf16[1,224,1536]{2,1,0:T(8,128)(2,1)} %param.4) | copy-start | bytes 2064388
  0.6 117.5 %copy-start = (f32[1,224,1536]{2,1,0:T(8,128)S(1)}, f32[1,224,1536]{2,1,0:T(8,128)}, u32[]{:S(2)}) copy-start(f32[1,224,1536]{2,1,0:T(8,128)} %param.3) | copy-start | bytes 4128772
  118.1 1.0 copy-start.2
  119.1 0.9 copy-start.3
  120.0 0.7 copy-start.4

commit v3 on v2

--- a/solution.py
+++ b/solution.py
@@ -16,11 +16,14 @@
 
 BLOCK = 128
 BLOCKS = COLS // BLOCK
-TILES = 5
-HALVES = 2
+SLOTS = 9
+SLOT = BLOCK + 8
+CHUNK = 4 * BLOCK + 8 + BLOCK // 2
 RING = 8
 LONG = RING // 2
 SHORT = RING - 1 - LONG
+
+LAST, HALF = "last", "half"
 
 keep_rate = 0.9
 epsilon = 1e-06
@@ -120,7 +123,6 @@
     near_in,
     near_out,
     tiles,
-    sib_tiles,
     w_high,
     w_mid,
     r_terms,
@@ -252,22 +254,81 @@
         for n, part in enumerate(split(blended.T, 2)):
             flat[b, BLOCK * n : BLOCK * (n + 1), :] = part
 
-    def place(chunk, of_core, s):
-        tile = TILES * (2 * chunk + of_core) + s
+    def place(chunk, slot):
+        tile = RING * slot + chunk
         row = lax.rem(tile, BLOCKS)
-        return row, lax.rem(row + tile // BLOCKS, BLOCKS)
-
-    def own_tile(store, chunk, s):
-        row, column = place(chunk, core, s)
+        return row, lax.rem(row + tile // BLOCKS + 1, BLOCKS)
+
+    def is_pair(chunk, of_core):
+        return of_core * ((chunk + 6) // RING)
+
+    tile_row = lax.broadcasted_iota(jnp.int32, (BLOCK, BLOCK), 0)
+    tile_column = lax.broadcasted_iota(jnp.int32, (BLOCK, BLOCK), 1)
+
+    def product(row, column):
         both = nn(flat[row], tall[column])
         part = lambda i, j: both[BLOCK * i : BLOCK * (i + 1), BLOCK * j : BLOCK * (j + 1)]
-        store[s] = part(0, 0) + (part(0, 1) + (part(1, 0) + part(1, 1)))
+        return part(0, 0) + (part(0, 1) + (part(1, 0) + part(1, 1)))
+
+    def own_terms(store, chunk, s):
+        if s is LAST:
+            pair = is_pair(chunk, core)
+            row, column = place(chunk, 3 + 5 * core)
+            first = product(
+                pair * (chunk - 2) + (1 - pair) * row, pair * (chunk - 2) + (1 - pair) * column
+            )
+            second = product(
+                pair * (chunk + 4) + (1 - pair) * row, pair * (chunk + 4) + (1 - pair) * column
+            )
+            store[3 * BLOCK : 4 * BLOCK] = jnp.where(
+                tile_row + (1 - pair) * BLOCK >= tile_column, first, second
+            )
+            diagonal = jnp.sum(
+                jnp.where(tile_row == tile_column, second, 0.0), axis=0, keepdims=True
+            )
+            store[4 * BLOCK : 4 * BLOCK + 8] = jnp.broadcast_to(diagonal, (8, BLOCK))
+        elif s is HALF:
+            row, column = place(chunk, 4)
+            start = pl.multiple_of(core * (BLOCK // 2), BLOCK // 2)
+            rows_of = [flat[row, pl.ds(BLOCK * n + start, BLOCK // 2)] for n in range(2)]
+            both = nn(jnp.concatenate(rows_of, axis=0), tall[column])
+            upper, lower = both[: BLOCK // 2], both[BLOCK // 2 :]
+            store[CHUNK - BLOCK // 2 :] = upper[:, :BLOCK] + (
+                upper[:, BLOCK:] + (lower[:, :BLOCK] + lower[:, BLOCK:])
+            )
+        else:
+            row, column = place(chunk, s + 5 * core)
+            store[pl.ds(pl.multiple_of(BLOCK * s, BLOCK), BLOCK)] = product(row, column)
 
     def at(steps):
         return lax.rem(chip + way * steps + RING, RING)
 
-    half = BLOCK // HALVES
-    halves = [(h, pl.ds(half * h, half)) for h in range(HALVES)]
+    def index(s):
+        return 3 if s is LAST else 4 if s is HALF else s
+
+    def part_of(s):
+        if s is LAST:
+            return pl.ds(3 * BLOCK, SLOT)
+        if s is HALF:
+            return pl.ds(CHUNK - BLOCK // 2, BLOCK // 2)
+        return pl.ds(pl.multiple_of(BLOCK * s, BLOCK), BLOCK)
+
+    def slot_rows(slot, size=BLOCK):
+        return pl.ds(pl.multiple_of(SLOT * slot, 8), size)
+
+    def finished(chunk, of_core, s):
+        if s is HALF:
+            start = pl.multiple_of(4 * SLOT + of_core * (BLOCK // 2), 8)
+            return tiles.at[chunk, pl.ds(start, BLOCK // 2)]
+        return tiles.at[chunk, slot_rows(index(s) + 5 * of_core, SLOT if s is LAST else BLOCK)]
+
+    def each(visit):
+        @pl.loop(0, 3)
+        def _(s):
+            visit(s)
+
+        visit(LAST)
+        visit(HALF)
 
     def remote(source, target, send, recv, device):
         return pltpu.make_async_remote_copy(
@@ -279,129 +340,144 @@
             device_id_type=MESH,
         )
 
-    def far_copy(step, s, h, rows):
+    def far_copy(step, s):
         return remote(
-            far_out.at[step, s, rows],
-            far_in.at[step, s, rows],
+            far_out.at[step, part_of(s)],
+            far_in.at[step, part_of(s)],
             ring_send.at[0],
-            far_recv.at[step, s, h],
+            far_recv.at[step, index(s)],
             ahead,
         )
 
-    def near_copy(step, s, h, rows):
+    def near_copy(step, s):
         return remote(
-            near_out.at[step, s, rows],
-            near_in.at[step, s, rows],
+            near_out.at[step, part_of(s)],
+            near_in.at[step, part_of(s)],
             ring_send.at[1],
-            near_recv.at[step, s, h],
+            near_recv.at[step, index(s)],
             behind,
         )
 
-    def gather_far(step, chunk, s, h, rows):
-        place_of = tiles.at[chunk, s, rows]
-        return remote(
-            place_of, place_of, gather_send.at[0], gather_far_recv.at[step, s, h], ahead
-        )
-
-    def gather_near(step, chunk, s, h, rows):
-        place_of = tiles.at[chunk, s, rows]
-        return remote(
-            place_of, place_of, gather_send.at[1], gather_near_recv.at[step, s, h], behind
-        )
-
-    def sib_copy(order, chunk, s, h, rows):
-        return remote(
-            tiles.at[chunk, s, rows],
-            sib_tiles.at[chunk, s, rows],
-            sib_send,
-            sib_recv.at[order, s, h],
-            sibling,
-        )
-
-    def expand(store, chunk, of_core, s):
-        row, column = place(chunk, of_core, s)
-        tile = store[chunk, s]
+    def gather_far(step, chunk, s):
+        view = finished(chunk, core, s)
+        return remote(view, view, gather_send.at[0], gather_far_recv.at[step, index(s)], ahead)
+
+    def gather_near(step, chunk, s):
+        view = finished(chunk, core, s)
+        return remote(view, view, gather_send.at[1], gather_near_recv.at[step, index(s)], behind)
+
+    def sib_copy(order, chunk, of_core, s):
+        view = finished(chunk, of_core, s)
+        return remote(view, view, sib_send, sib_recv.at[order, index(s)], sibling)
+
+    def store_tile(row, column, tile):
         for target, part in zip((w_high, w_mid), split(tile, 2)):
             target[row, column] = part
-        for target, part in zip((w_high, w_mid), split(tile.T, 2)):
-            target[column, row] = part
+
+    def expand_slot(chunk, slot):
+        row, column = place(chunk, slot)
+        tile = tiles[chunk, slot_rows(slot)]
+        store_tile(row, column, tile)
+        store_tile(column, row, tile.T)
+
+    def expand(chunk, of_core, s):
+        if s is not LAST:
+            expand_slot(chunk, s + 5 * of_core)
+            return
+        pair = is_pair(chunk, of_core)
+        slot = 3 + 5 * of_core
+
+        @pl.when(pair == 0)
+        def _():
+            expand_slot(chunk, slot)
+
+        @pl.when(pair == 1)
+        def _():
+            tile = tiles[chunk, slot_rows(slot)]
+            turned = tile.T
+            start = pl.multiple_of(SLOT * slot + BLOCK, 8)
+            diagonal = jnp.broadcast_to(tiles[chunk, pl.ds(start, 8)][0:1], (BLOCK, BLOCK))
+            store_tile(chunk - 2, chunk - 2, jnp.where(tile_row >= tile_column, tile, turned))
+            other = jnp.where(tile_row == tile_column, diagonal, turned)
+            store_tile(
+                chunk + 4, chunk + 4, jnp.where(tile_row < tile_column, tile, other)
+            )
 
     def sib_expand(order, s):
         steps = 0 if order == 0 else (order + 1) // 2 if order % 2 else -(order // 2)
-        for h, rows in halves:
-            sib_copy(order, at(steps), s, h, rows).wait_recv()
-        expand(sib_tiles, at(steps), 1 - core, s)
-
-    @pl.loop(0, TILES)
-    def _(s):
-        own_tile(own_far, at(LONG), s)
-        for h, rows in halves:
-            far_out[0, s, rows] = own_far[s, rows]
-            far_copy(0, s, h, rows).start()
-        own_tile(own_near, at(-SHORT), s)
-        for h, rows in halves:
-            near_out[0, s, rows] = own_near[s, rows]
-            near_copy(0, s, h, rows).start()
-
-    @pl.loop(0, TILES)
-    def _(s):
-        own_tile(own_far, at(LONG - 1), s)
-        own_tile(own_near, at(1 - SHORT), s)
+        sib_copy(order, at(steps), 1 - core, s).wait_recv()
+        if s is HALF:
+            expand_slot(at(steps), 4)
+        else:
+            expand(at(steps), 1 - core, s)
+
+    def start_ring(s):
+        own_terms(own_far, at(LONG), s)
+        far_out[0, part_of(s)] = own_far[part_of(s)]
+        far_copy(0, s).start()
+        own_terms(own_near, at(-SHORT), s)
+        near_out[0, part_of(s)] = own_near[part_of(s)]
+        near_copy(0, s).start()
+
+    def next_terms(s):
+        own_terms(own_far, at(LONG - 1), s)
+        own_terms(own_near, at(1 - SHORT), s)
+
+    each(start_ring)
+    each(next_terms)
+
+    def pass_on(step, s):
+        rows = part_of(s)
+        far_copy(step - 1, s).wait_recv()
+        far_out[step, rows] = own_far[rows] + far_in[step - 1, rows]
+        far_copy(step, s).start()
+        if step < SHORT:
+            near_copy(step - 1, s).wait_recv()
+            near_out[step, rows] = own_near[rows] + near_in[step - 1, rows]
+            near_copy(step, s).start()
+        own_terms(own_far, at(LONG - 1 - step), s)
+        if step < SHORT - 1:
+            own_terms(own_near, at(step + 1 - SHORT), s)
 
     for step in range(1, LONG):
-
-        @pl.loop(0, TILES)
-        def _(s):
-            for h, rows in halves:
-                far_copy(step - 1, s, h, rows).wait_recv()
-                far_out[step, s, rows] = own_far[s, rows] + far_in[step - 1, s, rows]
-                far_copy(step, s, h, rows).start()
-            own_tile(own_far, at(LONG - 1 - step), s)
+        each(functools.partial(pass_on, step))
+
+    def finish_sum(s):
+        rows = part_of(s)
+        near_copy(SHORT - 1, s).wait_recv()
+        far_copy(LONG - 1, s).wait_recv()
+        view = finished(chip, core, s)
+        view[...] = own_far[rows] + near_in[SHORT - 1, rows] + far_in[LONG - 1, rows]
+        gather_far(0, chip, s).start()
+        gather_near(0, chip, s).start()
+        sib_copy(0, chip, core, s).start()
+        if s is not HALF:
+            expand(chip, core, s)
+
+    each(finish_sum)
+
+    def spread(step, s):
+        from_behind, from_ahead = at(-1 - step), at(1 + step)
+        gather_far(step, from_behind, s).wait_recv()
+        if step < LONG - 1:
+            gather_far(step + 1, from_behind, s).start()
+        sib_copy(2 * step + 1, from_behind, core, s).start()
+        if step < SHORT:
+            gather_near(step, from_ahead, s).wait_recv()
+            if step < SHORT - 1:
+                gather_near(step + 1, from_ahead, s).start()
+            sib_copy(2 * step + 2, from_ahead, core, s).start()
+        if s is not HALF:
+            expand(from_behind, core, s)
             if step < SHORT:
-                for h, rows in halves:
-                    near_copy(step - 1, s, h, rows).wait_recv()
-                    near_out[step, s, rows] = own_near[s, rows] + near_in[step - 1, s, rows]
-                    near_copy(step, s, h, rows).start()
-                if step < SHORT - 1:
-                    own_tile(own_near, at(step + 1 - SHORT), s)
-
-    @pl.loop(0, TILES)
-    def _(s):
-        for h, rows in halves:
-            near_copy(SHORT - 1, s, h, rows).wait_recv()
-            far_copy(LONG - 1, s, h, rows).wait_recv()
-            tiles[chip, s, rows] = (
-                own_far[s, rows] + near_in[SHORT - 1, s, rows] + far_in[LONG - 1, s, rows]
-            )
-            gather_far(0, chip, s, h, rows).start()
-            gather_near(0, chip, s, h, rows).start()
-            sib_copy(0, chip, s, h, rows).start()
-        expand(tiles, chip, core, s)
+                expand(from_ahead, core, s)
+        for order in range(max(0, 2 * step - 1), 2 * step + 1):
+            sib_expand(order, s)
 
     for step in range(LONG):
-
-        @pl.loop(0, TILES)
-        def _(s):
-            from_behind, from_ahead = at(-1 - step), at(1 + step)
-            for h, rows in halves:
-                gather_far(step, from_behind, s, h, rows).wait_recv()
-                if step < LONG - 1:
-                    gather_far(step + 1, from_behind, s, h, rows).start()
-                sib_copy(2 * step + 1, from_behind, s, h, rows).start()
-            expand(tiles, from_behind, core, s)
-            if step < SHORT:
-                for h, rows in halves:
-                    gather_near(step, from_ahead, s, h, rows).wait_recv()
-                    if step < SHORT - 1:
-                        gather_near(step + 1, from_ahead, s, h, rows).start()
-                    sib_copy(2 * step + 2, from_ahead, s, h, rows).start()
-                expand(tiles, from_ahead, core, s)
-            for order in range(max(0, 2 * step - 1), 2 * step + 1):
-                sib_expand(order, s)
-
-    @pl.loop(0, TILES)
-    def _(s):
-        sib_expand(RING - 1, s)
+        each(functools.partial(spread, step))
+
+    each(functools.partial(sib_expand, RING - 1))
 
     def keep(values, target):
         for n, part in enumerate(split(values, 3)):
@@ -494,9 +570,9 @@
     for sent, semaphore in (
         (far_out, ring_send.at[0]),
         (near_out, ring_send.at[1]),
-        (tiles.at[pl.ds(0, LONG)], gather_send.at[0]),
-        (tiles.at[pl.ds(0, SHORT)], gather_send.at[1]),
-        (tiles, sib_send),
+        (far_out, gather_send.at[0]),
+        (near_out, gather_send.at[1]),
+        (tiles.at[:, pl.ds(0, CHUNK)], sib_send),
     ):
         pltpu.make_async_copy(sent, sent, semaphore).wait()
 
@@ -529,9 +605,9 @@
     left, r_t, clip = pl.pallas_call(
         functools.partial(refresh_kernel, dp_size, element_count),
         out_shape=[
-            jax.ShapeDtypeStruct((rows, 2 * RANK), F32),
-            jax.ShapeDtypeStruct((RANK, cols), F32),
-            jax.ShapeDtypeStruct((8, BLOCK), F32),
+            pltpu.VMEM((rows, 2 * RANK), F32),
+            pltpu.VMEM((RANK, cols), F32),
+            pltpu.VMEM((8, BLOCK), F32),
         ],
         in_specs=[hbm] * 3,
         out_specs=[vmem] * 3,
@@ -546,14 +622,13 @@
             pltpu.VMEM((dp_size, 8, BLOCK), F32),
             pltpu.VMEM((BLOCKS, 2 * rows, 2 * BLOCK), BF16),
             pltpu.VMEM((BLOCKS, 2 * BLOCK, 2 * rows), BF16),
-            pltpu.VMEM((TILES,) + tile, F32),
-            pltpu.VMEM((TILES,) + tile, F32),
-            pltpu.VMEM((LONG, TILES) + tile, F32),
-            pltpu.VMEM((LONG, TILES) + tile, F32),
-            pltpu.VMEM((SHORT, TILES) + tile, F32),
-            pltpu.VMEM((SHORT, TILES) + tile, F32),
-            pltpu.VMEM((RING, TILES) + tile, F32),
-            pltpu.VMEM((RING, TILES) + tile, F32),
+            pltpu.VMEM((CHUNK, BLOCK), F32),
+            pltpu.VMEM((CHUNK, BLOCK), F32),
+            pltpu.VMEM((LONG, CHUNK, BLOCK), F32),
+            pltpu.VMEM((LONG, CHUNK, BLOCK), F32),
+            pltpu.VMEM((SHORT, CHUNK, BLOCK), F32),
+            pltpu.VMEM((SHORT, CHUNK, BLOCK), F32),
+            pltpu.VMEM((RING, SLOTS * SLOT, BLOCK), F32),
             pltpu.VMEM((BLOCKS, BLOCKS) + tile, BF16),
             pltpu.VMEM((BLOCKS, BLOCKS) + tile, BF16),
             pltpu.VMEM((3 * RANK, cols), BF16),
@@ -566,13 +641,13 @@
             dma((2,)),
             dma((2,)),
             dma((2,)),
-            dma((LONG, TILES, HALVES)),
-            dma((SHORT, TILES, HALVES)),
+            dma((LONG, 5)),
+            dma((SHORT, 5)),
             dma((2,)),
-            dma((LONG, TILES, HALVES)),
-            dma((SHORT, TILES, HALVES)),
+            dma((LONG, 5)),
+            dma((SHORT, 5)),
             dma,
-            dma((RING, TILES, HALVES)),
+            dma((RING, 5)),
         ],
         compiler_params=pltpu.CompilerParams(
             collective_id=0, has_side_effects=True, vmem_limit_bytes=56 << 20

time: 123 us -> 115 us (0.935)
  Pallas kernels: 119 us -> 114 us
  local copies, waits for them, and re-layouts: 2.56 us -> 0.01 us
    pallas_call x1, Pallas kernels: 117 us -> 112 us  [body(): pl.pallas_call(functools.partial(refresh_kernel, dp_size, element_count),...]
    unnamed x10 -> x4, local copies, waits for them, and re-layouts: 2.56 us -> 0.01 us
where the time goes in v3:
time: 115 us
  Pallas kernels  114 us (99%)
    pallas_call x1, Pallas kernels, body(): pl.pallas_call(functools.partial(refresh_kernel, dp_size, element_count),...  112 us

profile of v3, /device:TPU:1, one launch (start us, length us, event | category | flops | bytes accessed | tf_op | source)
XLA Modules:
  0.0 114.6 jit_solution(5331512265758934866)
XLA Ops:
  0.6 0.0 copy-start.1
  0.6 0.0 copy-start
  0.7 112.0 %shard_map.58 = (f32[224,128]{1,0:T(8,128)S(1)}, f32[64,1536]{1,0:T(8,128)S(1)}, f32[8,128]{1,0:T(8,128)S(1)}) custom-call(f32[224,1536]{1,0:T(8,128)} %bitcast.10, bf16[224,1536]{1,0:T(8,128)(2,1)} %bitcast.12, f32[64,1536]{1,0:T(8,128)} %bitcast.14), custom_call_target="tpu_custom_call" | custom-call | tf_op jit(solution)/shard_map/pallas_call | solution.py:605
  112.6 0.0 copy-done.1
  112.6 0.0 copy-done
  112.6 2.0 %shard_map.59 = (f32[224,1536]{1,0:T(8,128)}, f32[64,1536]{1,0:T(8,128)}, bf16[224,1536]{1,0:T(8,128)(2,1)}) custom-call(f32[224,1536]{1,0:T(8,128)S(1)} %bitcast.11, bf16[224,1536]{1,0:T(8,128)(2,1)S(1)} %bitcast.13, f32[8,128]{1,0:T(8,128)S(1)} %get-tuple-element.9.clip_ref, f32[224,128]{1,0:T(8,128)S(1)} %get-tuple-element.10.left_ref, ...), custom_call_target="tpu_custom_call" | custom-call | tf_op jit(solution)/shard_map/pallas_call | solution.py:659
Async XLA Ops:
  0.6 112.0 %copy-start.1 = (bf16[1,224,1536]{2,1,0:T(8,128)(2,1)S(1)}, bf16[1,224,1536]{2,1,0:T(8,128)(2,1)}, u32[]{:S(2)}) copy-start(bf16[1,224,1536]{2,1,0:T(8,128)(2,1)} %param.4) | copy-start | bytes 2064388
  0.6 112.0 %copy-start = (f32[1,224,1536]{2,1,0:T(8,128)S(1)}, f32[1,224,1536]{2,1,0:T(8,128)}, u32[]{:S(2)}) copy-start(f32[1,224,1536]{2,1,0:T(8,128)} %param.3) | copy-start | bytes 4128772

commit v4 on v3

--- a/solution.py
+++ b/solution.py
@@ -49,7 +49,7 @@
     return parts
 
 
-def inverse_cholesky(gram, between=()):
+def inverse_cholesky(gram, lines, between=()):
     full = (8, 2 * RANK)
     ones = lax.broadcasted_iota(jnp.int32, (RANK, RANK), 0) == lax.broadcasted_iota(
         jnp.int32, (RANK, RANK), 1
@@ -60,12 +60,14 @@
     for p in range(RANK // 8):
         if p < len(between):
             between[p]()
-        panel = panels[p]
+        lines[p] = panels[p]
+        rows = [jnp.broadcast_to(lines[p, i : i + 1, :], full) for i in range(8)]
         entry = [[None] * 8 for _ in range(8)]
-        for i in range(8):
-            for j in range(i + 1):
-                entry[i][j] = jnp.broadcast_to(panel[i : i + 1, 8 * p + j : 8 * p + j + 1], full)
-        rows = [jnp.broadcast_to(panel[i : i + 1, :], full) for i in range(8)]
+        for j in range(8):
+            own = RANK // 8 + 8 * p + j
+            lines[own] = jnp.broadcast_to(panels[p][:, 8 * p + j : 8 * p + j + 1], full)
+            for i in range(j, 8):
+                entry[i][j] = jnp.broadcast_to(lines[own, i : i + 1, :], full)
         scale = [None] * 8
         factor = [[None] * 8 for _ in range(8)]
         for j in range(8):
@@ -90,10 +92,10 @@
                 column[j] = column[j] * scale[j]
                 for i in range(j + 1, 8):
                     column[i] = column[i] - factor[i][j] * column[j]
-            left = panels[q]
-            for j in range(8):
-                left = left - column[j] * rows[j]
-            panels[q] = left
+            terms = [column[j] * rows[j] for j in range(8)]
+            while len(terms) > 1:
+                terms = [terms[n] + terms[n + 1] for n in range(0, len(terms), 2)]
+            panels[q] = panels[q] - terms[0]
     return jnp.concatenate(panels, axis=0)[:, RANK:]
 
 
@@ -129,6 +131,8 @@
     z_terms,
     v_terms,
     v_ref,
+    raw,
+    lines,
     load,
     small_send,
     small_recv,
@@ -154,33 +158,33 @@
     behind = lax.rem(chip - way + RING, RING) * 2 + core
     rows = m_ref.shape[0]
 
-    barrier = pltpu.get_barrier_semaphore()
-
-    @pl.loop(1, etp_size)
-    def _(step):
-        pl.semaphore_signal(
-            barrier, inc=1, device_id={"etp": lax.rem(me + step, etp_size)}, device_id_type=MESH
-        )
-
-    @pl.loop(1, dp_size)
-    def _(step):
-        pl.semaphore_signal(
-            barrier, inc=1, device_id={"dp": lax.rem(dp + step, dp_size)}, device_id_type=MESH
-        )
-
     loads = [
         pltpu.make_async_copy(source, target, load.at[n])
         for n, (source, target) in enumerate(((g_hbm, g_ref), (m_hbm, m_ref), (q_hbm, q_ref)))
     ]
     for copy in loads:
         copy.start()
+    barrier = pltpu.get_barrier_semaphore()
+
+    @pl.loop(1, etp_size)
+    def _(step):
+        pl.semaphore_signal(
+            barrier, inc=1, device_id={"etp": lax.rem(me + step, etp_size)}, device_id_type=MESH
+        )
+
+    @pl.loop(1, dp_size)
+    def _(step):
+        pl.semaphore_signal(
+            barrier, inc=1, device_id={"dp": lax.rem(dp + step, dp_size)}, device_id_type=MESH
+        )
+
     loads[0].wait()
     wide[...] = g_ref[...].astype(F32)
     partial = jnp.zeros((8, BLOCK), F32)
     for b in range(BLOCKS):
         piece = wide[:, BLOCK * b : BLOCK * (b + 1)]
         partial = partial + jnp.sum((piece * piece).reshape(rows // 8, 8, BLOCK), axis=0)
-    sums[me] = partial
+    sums[me] = jnp.sum(partial, axis=0, keepdims=True)
     loads[1].wait()
     loads[2].wait()
 
@@ -238,7 +242,7 @@
     everything = totals[0]
     for n in range(1, dp_size):
         everything = everything + totals[n]
-    total_sq = jnp.sum(jnp.sum(everything, axis=0, keepdims=True), axis=1, keepdims=True)
+    total_sq = jnp.sum(everything, axis=1, keepdims=True)
     clip = jnp.minimum(1.0, lax.rsqrt(total_sq / element_count + epsilon))
     clip_out[...] = jnp.broadcast_to(clip, (8, BLOCK))
     for copy in copies:
@@ -251,8 +255,7 @@
         blended = jnp.concatenate([own, sib], axis=0)
         for n, part in enumerate(split(blended, 2)):
             tall[b, :, BLOCK * n : BLOCK * (n + 1)] = part
-        for n, part in enumerate(split(blended.T, 2)):
-            flat[b, BLOCK * n : BLOCK * (n + 1), :] = part
+            flat[b, BLOCK * n : BLOCK * (n + 1), :] = part.T
 
     def place(chunk, slot):
         tile = RING * slot + chunk
@@ -530,7 +533,7 @@
         for n in range(BLOCKS // 2):
             gram_columns(r_terms, n)
         keep(v_ref[...], z_terms)
-        inverse = inverse_cholesky(small_gram())
+        inverse = inverse_cholesky(small_gram(), lines)
         across = apply(inverse, z_terms)
         keep(across * normalise(across), r_terms)
 
@@ -542,6 +545,7 @@
     def _(turn):
         inverse = inverse_cholesky(
             small_gram(),
+            lines,
             [functools.partial(gram_columns, z_terms, n) for n in range(BLOCKS // 2)],
         )
         keep(v_ref[...], v_terms)
@@ -551,21 +555,36 @@
         keep(across * scale, r_terms)
         keep(ahead_of * scale, z_terms)
 
-    inverse = inverse_cholesky(small_gram())
+    def last_raw():
+        high, middle = (
+            jnp.concatenate(
+                [tall[b, :rows, BLOCK * n : BLOCK * (n + 1)] for b in range(BLOCKS)], axis=1
+            )
+            for n in range(2)
+        )
+        first = nt(high, r_terms[...])
+        second = nt(middle, r_terms[: 2 * RANK, :])
+        raw[...] = first[:, :RANK] + (
+            (first[:, RANK : 2 * RANK] + second[:, :RANK])
+            + (first[:, 2 * RANK :] + second[:, RANK:])
+        )
+
+    inverse = inverse_cholesky(small_gram(), lines, [last_raw])
+    both = nt(
+        jnp.concatenate(split(raw[...], 3), axis=0), jnp.concatenate(split(inverse, 3), axis=0)
+    )
+    part = lambda i, j: both[rows * i : rows * (i + 1), RANK * j : RANK * (j + 1)]
+    left = part(0, 0) + ((part(0, 1) + part(1, 0)) + (part(1, 1) + (part(0, 2) + part(2, 0))))
     across = apply(inverse, z_terms)
-    scale = normalise(across)
+    square = jnp.sum(across * across, axis=1, keepdims=True) + epsilon
+    scale = lax.rsqrt(square)
     r_out[...] = across * scale
-    left_map = apply(inverse, r_terms)
-    norm = scale * (jnp.sum(across * across, axis=1, keepdims=True) + epsilon)
-    maps = jnp.concatenate(split(left_map * norm, 2) + split(left_map, 2), axis=0)
-    blended = m_ref[...] + clip * wide[...]
-    both = nt(jnp.concatenate(split(blended, 2), axis=0), maps)
-    both = both[:rows] + both[rows:]
-    for n in range(2):
-        first = both[:, 2 * RANK * n : 2 * RANK * n + RANK]
-        left_out[:, RANK * n : RANK * (n + 1)] = (
-            first + both[:, 2 * RANK * n + RANK : 2 * RANK * (n + 1)]
-        )
+    same = lax.broadcasted_iota(jnp.int32, (RANK, RANK), 0) == lax.broadcasted_iota(
+        jnp.int32, (RANK, RANK), 1
+    )
+    norm = jnp.sum(jnp.where(same, square * scale, 0.0), axis=0, keepdims=True)
+    left_out[:, :RANK] = left * norm
+    left_out[:, RANK:] = left
 
     for sent, semaphore in (
         (far_out, ring_send.at[0]),
@@ -618,8 +637,8 @@
             pltpu.VMEM((rows, cols), F32),
             pltpu.VMEM((rows, cols), F32),
             pltpu.VMEM((rows, cols), F32),
-            pltpu.VMEM((2 * RING, 8, BLOCK), F32),
-            pltpu.VMEM((dp_size, 8, BLOCK), F32),
+            pltpu.VMEM((2 * RING, 1, BLOCK), F32),
+            pltpu.VMEM((dp_size, 1, BLOCK), F32),
             pltpu.VMEM((BLOCKS, 2 * rows, 2 * BLOCK), BF16),
             pltpu.VMEM((BLOCKS, 2 * BLOCK, 2 * rows), BF16),
             pltpu.VMEM((CHUNK, BLOCK), F32),
@@ -635,6 +654,8 @@
             pltpu.VMEM((3 * RANK, cols), BF16),
             pltpu.VMEM((3 * RANK, cols), BF16),
             pltpu.VMEM((RANK, cols), F32),
+            pltpu.VMEM((rows, RANK), F32),
+            pltpu.VMEM((RANK // 8 + RANK, 8, 2 * RANK), F32),
             dma((3,)),
             dma((2,)),
             dma((2,)),

time: 115 us -> 109 us (0.948)
  Pallas kernels: 114 us -> 109 us
    pallas_call x1, Pallas kernels: 112 us -> 107 us  [body(): pl.pallas_call(functools.partial(refresh_kernel, dp_size, element_count),...]
where the time goes in v4:
time: 109 us
  Pallas kernels  109 us (100%)
    pallas_call x1, Pallas kernels, body(): pl.pallas_call(functools.partial(refresh_kernel, dp_size, element_count),...  107 us

profile of v4, /device:TPU:1, one launch (start us, length us, event | category | flops | bytes accessed | tf_op | source)
XLA Modules:
  0.0 109.3 jit_solution(17203686621327145198)
XLA Ops:
  0.6 0.0 copy-start.1
  0.6 0.0 copy-start
  0.7 106.7 %shard_map.58 = (f32[224,128]{1,0:T(8,128)S(1)}, f32[64,1536]{1,0:T(8,128)S(1)}, f32[8,128]{1,0:T(8,128)S(1)}) custom-call(f32[224,1536]{1,0:T(8,128)} %bitcast.10, bf16[224,1536]{1,0:T(8,128)(2,1)} %bitcast.12, f32[64,1536]{1,0:T(8,128)} %bitcast.14), custom_call_target="tpu_custom_call" | custom-call | tf_op jit(solution)/shard_map/pallas_call | solution.py:624
  107.3 0.0 copy-done.1
  107.4 0.0 copy-done
  107.4 2.0 %shard_map.59 = (f32[224,1536]{1,0:T(8,128)}, f32[64,1536]{1,0:T(8,128)}, bf16[224,1536]{1,0:T(8,128)(2,1)}) custom-call(f32[224,1536]{1,0:T(8,128)S(1)} %bitcast.11, bf16[224,1536]{1,0:T(8,128)(2,1)S(1)} %bitcast.13, f32[8,128]{1,0:T(8,128)S(1)} %get-tuple-element.9.clip_ref, f32[224,128]{1,0:T(8,128)S(1)} %get-tuple-element.10.left_ref, ...), custom_call_target="tpu_custom_call" | custom-call | tf_op jit(solution)/shard_map/pallas_call | solution.py:680
Async XLA Ops:
  0.6 106.7 %copy-start.1 = (bf16[1,224,1536]{2,1,0:T(8,128)(2,1)S(1)}, bf16[1,224,1536]{2,1,0:T(8,128)(2,1)}, u32[]{:S(2)}) copy-start(bf16[1,224,1536]{2,1,0:T(8,128)(2,1)} %param.4) | copy-start | bytes 2064388
  0.6 106.7 %copy-start = (f32[1,224,1536]{2,1,0:T(8,128)S(1)}, f32[1,224,1536]{2,1,0:T(8,128)}, u32[]{:S(2)}) copy-start(f32[1,224,1536]{2,1,0:T(8,128)} %param.3) | copy-start | bytes 4128772

commit v5 on v4

--- a/solution.py
+++ b/solution.py
@@ -57,17 +57,31 @@
     joined = jnp.concatenate([gram, ones.astype(F32)], axis=1)
     panels = [joined[8 * p : 8 * p + 8] for p in range(RANK // 8)]
     sublane = lax.broadcasted_iota(jnp.int32, full, 0)
+
+    def across_lanes(values, first):
+        return [
+            jnp.broadcast_to(values[:, first + j : first + j + 1], full) for j in range(8)
+        ]
+
+    def line(at, values, i):
+        if i == 0:
+            lines[at] = values
+        return jnp.broadcast_to(lines[at, i : i + 1, :], full)
+
+    diagonal = across_lanes(panels[0], 0)
     for p in range(RANK // 8):
         if p < len(between):
             between[p]()
-        lines[p] = panels[p]
-        rows = [jnp.broadcast_to(lines[p, i : i + 1, :], full) for i in range(8)]
+        start = 17 * p
+        rows = [line(start, panels[p], i) for i in range(8)]
         entry = [[None] * 8 for _ in range(8)]
         for j in range(8):
-            own = RANK // 8 + 8 * p + j
-            lines[own] = jnp.broadcast_to(panels[p][:, 8 * p + j : 8 * p + j + 1], full)
-            for i in range(j, 8):
-                entry[i][j] = jnp.broadcast_to(lines[own, i : i + 1, :], full)
+            for i in range(8):
+                entry[i][j] = line(start + 1 + j, diagonal[j], i)
+        ahead = p + 1 < RANK // 8
+        if ahead:
+            beside = across_lanes(panels[p + 1], 8 * p)
+            diagonal = across_lanes(panels[p + 1], 8 * p + 8)
         scale = [None] * 8
         factor = [[None] * 8 for _ in range(8)]
         for j in range(8):
@@ -77,6 +91,12 @@
             for i in range(j + 1, 8):
                 for m in range(j + 1, i + 1):
                     entry[i][m] = entry[i][m] - factor[i][j] * factor[m][j]
+            if ahead:
+                beside[j] = beside[j] * scale[j]
+                for i in range(j + 1, 8):
+                    beside[i] = beside[i] - factor[i][j] * beside[j]
+                for i in range(8):
+                    diagonal[i] = diagonal[i] - beside[j] * line(start + 9 + j, beside[j], i)
             rows[j] = rows[j] * scale[j]
             for i in range(j + 1, 8):
                 rows[i] = rows[i] - factor[i][j] * rows[j]
@@ -85,14 +105,14 @@
             done = jnp.where(sublane == i, rows[i], done)
         panels[p] = done
         for q in range(p + 1, RANK // 8):
-            column = [
-                jnp.broadcast_to(panels[q][:, 8 * p + j : 8 * p + j + 1], full) for j in range(8)
-            ]
-            for j in range(8):
-                column[j] = column[j] * scale[j]
-                for i in range(j + 1, 8):
-                    column[i] = column[i] - factor[i][j] * column[j]
-            terms = [column[j] * rows[j] for j in range(8)]
+            columns = beside
+            if q > p + 1:
+                columns = across_lanes(panels[q], 8 * p)
+                for j in range(8):
+                    columns[j] = columns[j] * scale[j]
+                    for i in range(j + 1, 8):
+                        columns[i] = columns[i] - factor[i][j] * columns[j]
+            terms = [columns[j] * rows[j] for j in range(8)]
             while len(terms) > 1:
                 terms = [terms[n] + terms[n + 1] for n in range(0, len(terms), 2)]
             panels[q] = panels[q] - terms[0]
@@ -655,7 +675,7 @@
             pltpu.VMEM((3 * RANK, cols), BF16),
             pltpu.VMEM((RANK, cols), F32),
             pltpu.VMEM((rows, RANK), F32),
-            pltpu.VMEM((RANK // 8 + RANK, 8, 2 * RANK), F32),
+            pltpu.VMEM((17 * RANK // 8, 8, 2 * RANK), F32),
             dma((3,)),
             dma((2,)),
             dma((2,)),

time: 109 us -> 107 us (0.982)
  Pallas kernels: 109 us -> 106 us
    pallas_call x1, Pallas kernels: 107 us -> 104 us  [body(): pl.pallas_call(functools.partial(refresh_kernel, dp_size, element_count),...]
where the time goes in v5:
time: 107 us
  Pallas kernels  106 us (99%)
    pallas_call x1, Pallas kernels, body(): pl.pallas_call(functools.partial(refresh_kernel, dp_size, element_count),...  104 us

profile of v5, /device:TPU:1, one launch (start us, length us, event | category | flops | bytes accessed | tf_op | source)
XLA Modules:
  0.0 107.1 jit_solution(12723190243831541961)
XLA Ops:
  0.6 0.0 copy-start.1
  0.6 0.0 copy-start
  0.7 104.4 %shard_map.58 = (f32[224,128]{1,0:T(8,128)S(1)}, f32[64,1536]{1,0:T(8,128)S(1)}, f32[8,128]{1,0:T(8,128)S(1)}) custom-call(f32[224,1536]{1,0:T(8,128)} %bitcast.10, bf16[224,1536]{1,0:T(8,128)(2,1)} %bitcast.12, f32[64,1536]{1,0:T(8,128)} %bitcast.14), custom_call_target="tpu_custom_call" | custom-call | tf_op jit(solution)/shard_map/pallas_call | solution.py:644
  105.1 0.0 copy-done.1
  105.1 0.0 copy-done
  105.1 2.0 %shard_map.59 = (f32[224,1536]{1,0:T(8,128)}, f32[64,1536]{1,0:T(8,128)}, bf16[224,1536]{1,0:T(8,128)(2,1)}) custom-call(f32[224,1536]{1,0:T(8,128)S(1)} %bitcast.11, bf16[224,1536]{1,0:T(8,128)(2,1)S(1)} %bitcast.13, f32[8,128]{1,0:T(8,128)S(1)} %get-tuple-element.9.clip_ref, f32[224,128]{1,0:T(8,128)S(1)} %get-tuple-element.10.left_ref, ...), custom_call_target="tpu_custom_call" | custom-call | tf_op jit(solution)/shard_map/pallas_call | solution.py:700
Async XLA Ops:
  0.6 104.4 %copy-start.1 = (bf16[1,224,1536]{2,1,0:T(8,128)(2,1)S(1)}, bf16[1,224,1536]{2,1,0:T(8,128)(2,1)}, u32[]{:S(2)}) copy-start(bf16[1,224,1536]{2,1,0:T(8,128)(2,1)} %param.4) | copy-start | bytes 2064388
  0.6 104.4 %copy-start = (f32[1,224,1536]{2,1,0:T(8,128)S(1)}, f32[1,224,1536]{2,1,0:T(8,128)}, u32[]{:S(2)}) copy-start(f32[1,224,1536]{2,1,0:T(8,128)} %param.3) | copy-start | bytes 4128772
